TPU v7x, 128 devices: a whole 4x4x4 slice. The times are simulated.
128 devices in a mesh: rep: 8 (over y_hi, z), shard: 16 (over y_lo, x, core).
Axes of the slice: x: 4, y: 4 (y_hi: 2, y_lo: 2; y = y_hi * 2 + y_lo), z: 4, core: 2. Of those that a mesh axis runs over, the one named last changes fastest.
Arguments:
- block_input: bfloat16 [32768, 1024], P(('rep', 'shard')), may hold values from -6 to 6
- cotangent: bfloat16 [32768, 1024], P(('rep', 'shard')), may hold values from -6 to 6
- routes: int32 [32768, 8], P(('rep', 'shard')), may hold values from 0 to 31, all different within a row; in each aligned block of 128 rows (0 to 127, 128 to 255, ...) at most 44 rows name the same one
- lengths: int32 [8, 2, 8], P('rep'), may hold values from 1 to 1024, 2048 in all within a row
- stream_slot: int32 [8, 2, 2048], P('rep'), may hold values from 0 to 2047, as said below
- w_qkv: bfloat16 [1024, 2048], P('shard'), may hold values from -0.1875 to 0.1875
- w_out: bfloat16 [1024, 1024], P('shard'), may hold values from -0.375 to 0.375
- w_router: bfloat16 [1024, 32], P('shard'), may hold values from -0.09375 to 0.09375
- g_attn: bfloat16 [1024], P('shard'), may hold values from 0.25 to 1.75
- g_moe: bfloat16 [1024], P('shard'), may hold values from 0.25 to 1.75
- g_q: bfloat16 [64], P('shard'), may hold values from 0.25 to 1.75
- g_k: bfloat16 [64], P('shard'), may hold values from 0.25 to 1.75
- w_gate: bfloat16 [32, 1024, 512], P('shard'), may hold values from -0.1875 to 0.1875
- w_up: bfloat16 [32, 1024, 512], P('shard'), may hold values from -0.1875 to 0.1875
- w_down: bfloat16 [32, 512, 1024], P('shard'), may hold values from -0.5 to 0.5
Outputs:
- mixed: bfloat16 [32768, 1024], P(('rep', 'shard'))
- grad_input: bfloat16 [32768, 1024], P(('rep', 'shard'))
- grad_qkv: float32 [1024, 2048], P('shard')
- grad_out: float32 [1024, 1024], P('shard')
- grad_router: float32 [1024, 32], P('shard')
- grad_attn_gain: float32 [1024], P('shard')
- grad_moe_gain: float32 [1024], P('shard')
- grad_q_gain: float32 [64], P('shard')
- grad_k_gain: float32 [64], P('shard')
- grad_gate: float32 [32, 1024, 512], P('shard')
- grad_up: float32 [32, 1024, 512], P('shard')
- grad_down: float32 [32, 512, 1024], P('shard')
Inputs may be any that keep to these rules, and one draw needn't show every extreme that they name: `routes`: in each aligned block of 128 rows (the rows of one device in one micro-batch) no expert is named more than 44 times, a bound that some block reaches; a row names 8 different experts. Each row of 8 lengths sums to 2048; its longest is 1024. `stream_slot`: for each group and micro-batch the 2048 entries are a permutation of the stream positions.
All inputs are finite; a program needn't handle non-finite values.
Results may differ from a plain program's by a relative error of at most 0.019.
Values may be sent and summed in bfloat16 or wider, within the bound.
No kernel may reach another device: no remote copies, remote signals or barrier semaphores. Data moves between devices by JAX's collectives and lax.ppermute only.
A program may use at most 256 MiB of HBM per device.

v0:
```python
import jax
import jax.numpy as jnp
from jax import lax
from jax.sharding import PartitionSpec as P

D = 1024
HEADS = 16
KV_HEADS = 8
HD = 64
TOP = 8
MICRO = 2


EPS = 1e-06


def rms_scale(values):
    return lax.rsqrt(jnp.mean(values * values, axis=-1, keepdims=True) + EPS)


def norm_back(grad_hat, normed, scale_values):
    return scale_values * (grad_hat - normed * jnp.mean(grad_hat * normed, axis=-1, keepdims=True))


def seq_tables(stream, seq_lens):
    ends = jnp.cumsum(seq_lens)
    after = (stream[:, None] >= ends[None, :]).astype(jnp.int32)
    seq_id = jnp.sum(after, axis=1)
    position = stream - jnp.sum(after * seq_lens[None, :], axis=1)
    return (seq_id, position)


def turn(values, position, direction):
    half = values.shape[-1] // 2
    freq = 10000.0 ** (-2.0 * jnp.arange(half, dtype=jnp.float32) / values.shape[-1])
    angle = position.astype(jnp.float32)[:, None] * freq[None, :]
    cosine = jnp.cos(angle)[:, None, :]
    sine = direction * jnp.sin(angle)[:, None, :]
    first = values[..., :half]
    second = values[..., half:]
    return jnp.concatenate(
        [first * cosine - second * sine, second * cosine + first * sine], axis=-1
    )


def route_slots(route_block, experts):
    expert_ids = route_block.reshape(-1)
    hits = (expert_ids[:, None] == jnp.arange(experts)[None, :]).astype(jnp.int32)
    before = jnp.cumsum(hits, axis=0) - hits
    return (expert_ids, jnp.sum(before * hits, axis=1))


def expert_front(received, w_gate, w_up):
    gate_part = jnp.einsum("sjcd,jdf->sjcf", received, w_gate, preferred_element_type=jnp.float32)
    up_part = jnp.einsum("sjcd,jdf->sjcf", received, w_up, preferred_element_type=jnp.float32)
    return (gate_part, up_part)


def local(
    block_input,
    cotangent,
    routes,
    lengths,
    stream_slot,
    w_qkv,
    w_out,
    w_router,
    g_attn,
    g_moe,
    g_q,
    g_k,
    w_gate,
    w_up,
    w_down,
):
    batch_rows = block_input.shape[0] // MICRO
    experts = w_router.shape[1]
    local_experts = w_gate.shape[0]
    capacity = batch_rows * TOP // experts * 11 // 8
    shards = lax.axis_size("shard")
    device = lax.axis_index("shard")
    all_rows = shards * batch_rows
    q_width = HEADS * HD
    kv_width = KV_HEADS * HD
    group_size = HEADS // KV_HEADS
    score_scale = HD ** (-0.5)
    front_totals = (
        jnp.zeros((D, q_width + 2 * kv_width), jnp.float32),
        jnp.zeros((q_width, D), jnp.float32),
        jnp.zeros((D, experts), jnp.float32),
        jnp.zeros((D,), jnp.float32),
        jnp.zeros((D,), jnp.float32),
        jnp.zeros((HD,), jnp.float32),
        jnp.zeros((HD,), jnp.float32),
    )
    grad_gate = jnp.zeros(w_gate.shape, jnp.float32)
    grad_up = jnp.zeros(w_up.shape, jnp.float32)
    grad_down = jnp.zeros(w_down.shape, jnp.float32)
    outputs = []
    input_grads = []
    for batch_index in range(MICRO):
        qkv_full, out_full, router_full, attn_gain, moe_gain, query_gain, key_gain = (
            lax.all_gather(w_qkv, "shard", axis=0, tiled=True),
            lax.all_gather(w_out, "shard", axis=0, tiled=True),
            lax.all_gather(w_router, "shard", axis=0, tiled=True),
            lax.all_gather(g_attn, "shard", axis=0, tiled=True),
            lax.all_gather(g_moe, "shard", axis=0, tiled=True),
            lax.all_gather(g_q, "shard", axis=0, tiled=True),
            lax.all_gather(g_k, "shard", axis=0, tiled=True),
        )
        attn_gain = attn_gain.astype(jnp.float32)
        moe_gain = moe_gain.astype(jnp.float32)
        query_gain = query_gain.astype(jnp.float32)
        key_gain = key_gain.astype(jnp.float32)
        lower = batch_index * batch_rows
        row_values = block_input[lower : lower + batch_rows].astype(jnp.float32)
        seq_all, position_all = seq_tables(stream_slot[0, batch_index], lengths[0, batch_index])
        seq_here = lax.dynamic_slice_in_dim(seq_all, device * batch_rows, batch_rows)
        position = lax.dynamic_slice_in_dim(position_all, device * batch_rows, batch_rows)
        attn_scale = rms_scale(row_values)
        attn_hat = row_values * attn_scale
        attn_in = (attn_hat * attn_gain).astype(jnp.bfloat16)
        projected = jnp.dot(attn_in, qkv_full, preferred_element_type=jnp.float32)
        query_raw = projected[:, :q_width].reshape(batch_rows, HEADS, HD)
        key_raw = projected[:, q_width : q_width + kv_width].reshape(batch_rows, KV_HEADS, HD)
        values = projected[:, q_width + kv_width :].astype(jnp.bfloat16)
        query_scale = rms_scale(query_raw)
        query_hat = query_raw * query_scale
        queries = turn(query_hat * query_gain, position, 1.0).astype(jnp.bfloat16)
        key_scale = rms_scale(key_raw)
        key_hat = key_raw * key_scale
        keys_flat = (
            turn(key_hat * key_gain, position, 1.0)
            .astype(jnp.bfloat16)
            .reshape(batch_rows, kv_width)
        )
        gathered_keys, gathered_values = (
            lax.all_gather(keys_flat, "shard", axis=0, tiled=True),
            lax.all_gather(values, "shard", axis=0, tiled=True),
        )
        key_block = gathered_keys.reshape(all_rows, KV_HEADS, HD)
        value_block = gathered_values.reshape(all_rows, KV_HEADS, HD)
        query_group = queries.reshape(batch_rows, KV_HEADS, group_size, HD)
        same_seq = seq_here[:, None] == seq_all[None, :]
        scores = (
            jnp.einsum("qhgd,khd->hgqk", query_group, key_block, preferred_element_type=jnp.float32)
            * score_scale
        )
        scores = jnp.where(same_seq[None, None], scores, -1e30)
        row_max = jnp.max(scores, axis=-1, keepdims=True)
        exp_scores = jnp.exp(scores - row_max)
        row_total = jnp.sum(exp_scores, axis=-1, keepdims=True)
        log_total = row_max + jnp.log(row_total)
        low_probs = (exp_scores / row_total).astype(jnp.bfloat16)
        attended = jnp.einsum(
            "hgqk,khd->qhgd", low_probs, value_block, preferred_element_type=jnp.float32
        )
        attended = attended.reshape(batch_rows, q_width).astype(jnp.bfloat16)
        mid = row_values + jnp.dot(attended, out_full, preferred_element_type=jnp.float32)
        moe_scale = rms_scale(mid)
        moe_hat = mid * moe_scale
        moe_in = (moe_hat * moe_gain).astype(jnp.bfloat16)
        logits = jnp.dot(moe_in, router_full, preferred_element_type=jnp.float32)
        route_here = routes[lower : lower + batch_rows]
        chosen_hot = (route_here[:, :, None] == jnp.arange(experts)[None, None, :]).astype(
            jnp.float32
        )
        gate_probs = jax.nn.softmax(jnp.sum(chosen_hot * logits[:, None, :], axis=-1), axis=-1)
        expert_ids, slot_index = route_slots(route_here, experts)
        token_index = jnp.arange(batch_rows * TOP) // TOP
        dispatch = (
            jnp.zeros((experts, capacity, D), jnp.bfloat16)
            .at[expert_ids, slot_index]
            .set(moe_in[token_index])
        )
        dispatch = dispatch.reshape(shards, local_experts, capacity, D)
        received = lax.all_to_all(dispatch, "shard", split_axis=0, concat_axis=0, tiled=True)
        gate_part, up_part = expert_front(received, w_gate, w_up)
        hidden = (jax.nn.silu(gate_part) * up_part).astype(jnp.bfloat16)
        produced = jnp.einsum(
            "sjcf,jfd->sjcd", hidden, w_down, preferred_element_type=jnp.float32
        ).astype(jnp.bfloat16)
        returned = lax.all_to_all(produced, "shard", split_axis=0, concat_axis=0, tiled=True)
        carried = (returned, received)
        returned = carried[0]
        received = carried[1]
        picked = (
            returned.reshape(experts, capacity, D)[expert_ids, slot_index]
            .reshape(batch_rows, TOP, D)
            .astype(jnp.float32)
        )
        mixed = mid + jnp.sum(gate_probs[:, :, None] * picked, axis=1)
        outputs.append(mixed.astype(jnp.bfloat16))
        upstream = cotangent[lower : lower + batch_rows].astype(jnp.float32)
        gate_grads = jnp.sum(upstream[:, None, :] * picked, axis=-1)
        chosen_grads = gate_probs * (
            gate_grads - jnp.sum(gate_probs * gate_grads, axis=-1, keepdims=True)
        )
        logit_grads = jnp.sum(chosen_hot * chosen_grads[:, :, None], axis=1).astype(jnp.bfloat16)
        pair_grads = (
            (gate_probs[:, :, None] * upstream[:, None, :])
            .astype(jnp.bfloat16)
            .reshape(batch_rows * TOP, D)
        )
        grad_dispatch = (
            jnp.zeros((experts, capacity, D), jnp.bfloat16)
            .at[expert_ids, slot_index]
            .set(pair_grads)
        )
        grad_received = lax.all_to_all(
            grad_dispatch.reshape(shards, local_experts, capacity, D),
            "shard",
            split_axis=0,
            concat_axis=0,
            tiled=True,
        )
        gate_part, up_part = expert_front(received, w_gate, w_up)
        activated = jax.nn.silu(gate_part)
        hidden = (activated * up_part).astype(jnp.bfloat16)
        grad_down = grad_down + jnp.einsum(
            "sjcf,sjcd->jfd", hidden, grad_received, preferred_element_type=jnp.float32
        )
        grad_hidden = jnp.einsum(
            "sjcd,jfd->sjcf", grad_received, w_down, preferred_element_type=jnp.float32
        )
        sigmoid_gate = jax.nn.sigmoid(gate_part)
        grad_gate_part = (
            grad_hidden * up_part * (sigmoid_gate + gate_part * sigmoid_gate * (1.0 - sigmoid_gate))
        ).astype(jnp.bfloat16)
        grad_up_part = (grad_hidden * activated).astype(jnp.bfloat16)
        grad_gate = grad_gate + jnp.einsum(
            "sjcd,sjcf->jdf", received, grad_gate_part, preferred_element_type=jnp.float32
        )
        grad_up = grad_up + jnp.einsum(
            "sjcd,sjcf->jdf", received, grad_up_part, preferred_element_type=jnp.float32
        )
        grad_rows_back = (
            jnp.einsum("sjcf,jdf->sjcd", grad_gate_part, w_gate, preferred_element_type=jnp.float32)
            + jnp.einsum("sjcf,jdf->sjcd", grad_up_part, w_up, preferred_element_type=jnp.float32)
        ).astype(jnp.bfloat16)
        grad_returned = lax.all_to_all(
            grad_rows_back, "shard", split_axis=0, concat_axis=0, tiled=True
        )
        grad_moe_in = jnp.sum(
            grad_returned.reshape(experts, capacity, D)[expert_ids, slot_index]
            .reshape(batch_rows, TOP, D)
            .astype(jnp.float32),
            axis=1,
        )
        grad_moe_in = grad_moe_in + jnp.einsum(
            "te,de->td", logit_grads, router_full, preferred_element_type=jnp.float32
        )
        batch_router = jnp.einsum(
            "td,te->de", moe_in, logit_grads, preferred_element_type=jnp.float32
        )
        batch_moe_gain = jnp.sum(grad_moe_in * moe_hat, axis=0)
        grad_mid = upstream + norm_back(grad_moe_in * moe_gain, moe_hat, moe_scale)
        grad_mid_low = grad_mid.astype(jnp.bfloat16)
        batch_out = jnp.einsum(
            "tq,td->qd", attended, grad_mid_low, preferred_element_type=jnp.float32
        )
        grad_attended = jnp.einsum(
            "td,qd->tq", grad_mid_low, out_full, preferred_element_type=jnp.float32
        )
        grad_attended = grad_attended.astype(jnp.bfloat16).reshape(
            batch_rows, KV_HEADS, group_size, HD
        )
        scores = (
            jnp.einsum("qhgd,khd->hgqk", query_group, key_block, preferred_element_type=jnp.float32)
            * score_scale
        )
        scores = jnp.where(same_seq[None, None], scores, -1e30)
        probs = jnp.exp(scores - log_total)
        low_probs = probs.astype(jnp.bfloat16)
        grad_probs = jnp.einsum(
            "qhgd,khd->hgqk", grad_attended, value_block, preferred_element_type=jnp.float32
        )
        row_dot = jnp.sum(probs * grad_probs, axis=-1, keepdims=True)
        grad_scores = (probs * (grad_probs - row_dot)).astype(jnp.bfloat16)
        grad_queries = (
            jnp.einsum("hgqk,khd->qhgd", grad_scores, key_block, preferred_element_type=jnp.float32)
            * score_scale
        )
        key_grad = (
            jnp.einsum(
                "hgqk,qhgd->khd", grad_scores, query_group, preferred_element_type=jnp.float32
            )
            * score_scale
        )
        value_grad = jnp.einsum(
            "hgqk,qhgd->khd", low_probs, grad_attended, preferred_element_type=jnp.float32
        )
        kv_grads = lax.psum_scatter(
            jnp.concatenate(
                [
                    key_grad.reshape(lax.axis_size("shard") * batch_rows, kv_width),
                    value_grad.reshape(lax.axis_size("shard") * batch_rows, kv_width),
                ],
                axis=1,
            ),
            "shard",
            scatter_dimension=0,
            tiled=True,
        )
        grad_query_normed = turn(grad_queries.reshape(batch_rows, HEADS, HD), position, -1.0)
        grad_key_normed = turn(
            kv_grads[:, :kv_width].reshape(batch_rows, KV_HEADS, HD), position, -1.0
        )
        batch_q_gain = jnp.sum(grad_query_normed * query_hat, axis=(0, 1))
        batch_k_gain = jnp.sum(grad_key_normed * key_hat, axis=(0, 1))
        grad_query_raw = norm_back(grad_query_normed * query_gain, query_hat, query_scale)
        grad_key_raw = norm_back(grad_key_normed * key_gain, key_hat, key_scale)
        grad_projected = jnp.concatenate(
            [
                grad_query_raw.reshape(batch_rows, q_width),
                grad_key_raw.reshape(batch_rows, kv_width),
                kv_grads[:, kv_width:],
            ],
            axis=1,
        ).astype(jnp.bfloat16)
        batch_qkv = jnp.einsum(
            "td,tc->dc", attn_in, grad_projected, preferred_element_type=jnp.float32
        )
        grad_attn_in = jnp.einsum(
            "tc,dc->td", grad_projected, qkv_full, preferred_element_type=jnp.float32
        )
        batch_attn_gain = jnp.sum(grad_attn_in * attn_hat, axis=0)
        grad_rows = grad_mid + norm_back(grad_attn_in * attn_gain, attn_hat, attn_scale)
        input_grads.append(grad_rows.astype(jnp.bfloat16))
        front_totals = tuple(
            (
                total + term
                for total, term in zip(
                    front_totals,
                    (
                        batch_qkv,
                        batch_out,
                        batch_router,
                        batch_attn_gain,
                        batch_moe_gain,
                        batch_q_gain,
                        batch_k_gain,
                    ),
                )
            )
        )
    owned = (
        lax.psum_scatter(front_totals[0], "shard", scatter_dimension=0, tiled=True),
        lax.psum_scatter(front_totals[1], "shard", scatter_dimension=0, tiled=True),
        lax.psum_scatter(front_totals[2], "shard", scatter_dimension=0, tiled=True),
        lax.psum_scatter(front_totals[3], "shard", scatter_dimension=0, tiled=True),
        lax.psum_scatter(front_totals[4], "shard", scatter_dimension=0, tiled=True),
        lax.psum_scatter(front_totals[5], "shard", scatter_dimension=0, tiled=True),
        lax.psum_scatter(front_totals[6], "shard", scatter_dimension=0, tiled=True),
    )
    summed = lax.psum(
        (
            owned[0],
            owned[1],
            owned[2],
            owned[3],
            owned[4],
            owned[5],
            owned[6],
            grad_gate,
            grad_up,
            grad_down,
        ),
        "rep",
    )
    return (
        jnp.concatenate(outputs, axis=0),
        jnp.concatenate(input_grads, axis=0),
        summed[0],
        summed[1],
        summed[2],
        summed[3],
        summed[4],
        summed[5],
        summed[6],
        summed[7],
        summed[8],
        summed[9],
    )


def solution(mesh):
    return jax.shard_map(
        local,
        mesh=mesh,
        in_specs=(
            P(("rep", "shard"), None),
            P(("rep", "shard"), None),
            P(("rep", "shard"), None),
            P("rep", None, None),
            P("rep", None, None),
            P("shard", None),
            P("shard", None),
            P("shard", None),
            P("shard"),
            P("shard"),
            P("shard"),
            P("shard"),
            P("shard", None, None),
            P("shard", None, None),
            P("shard", None, None),
        ),
        out_specs=(
            P(("rep", "shard"), None),
            P(("rep", "shard"), None),
            P("shard", None),
            P("shard", None),
            P("shard", None),
            P("shard"),
            P("shard"),
            P("shard"),
            P("shard"),
            P("shard", None, None),
            P("shard", None, None),
            P("shard", None, None),
        ),
        check_vma=False,
    )
```

profile of v0, /device:TPU:1, one launch (start us, length us, event | category | flops | bytes accessed | tf_op | source)
XLA Modules:
  0.0 1468.6 jit_solution(10980264594730388457)
XLA Ops:
  14.0 29.0 %all-reduce.11 = (bf16[1024]{0:T(1024)(128)(2,1)S(1)}, bf16[64]{0:T(256)(128)(2,1)S(1)}, bf16[64]{0:T(256)(128)(2,1)S(1)}, bf16[1024]{0:T(1024)(128)(2,1)S(1)}) all-reduce(bf16[1024]{0:T(1024)(128)(2,1)S(1)} %dynamic-update-slice, bf16[64]{0:T(256)(128)(2,1)S(1)} %dynamic-update-slice.1, ...), channel_id=1, replica_groups=mesh['rep'=8,'shard'=16] {'shard'}, use_global_device_ids=true, to_apply=%add | all-reduce | flops 2176 | bytes 8704
  73.5 9.0 reduce-window.40
  99.1 10.0 fusion.174
  117.8 17.4 %all-gather.10.cloned.1.call-done = bf16[2048,512]{1,0:T(8,128)(2,1)} async-done(((bf16[128,512]{1,0:T(8,128)(2,1)}), bf16[2048,512]{1,0:T(8,128)(2,1)}) %all-gather.10.cloned.1.call-update) | async-done | bytes 2097168 | tf_op jit(solution)/shard_map/all_gather | solution.py:139
  139.1 9.2 fusion.101
  148.3 22.4 %all-gather.14.cloned.1.call-done = bf16[1024,1024]{1,0:T(8,128)(2,1)} async-done(((bf16[64,1024]{1,0:T(8,128)(2,1)}), bf16[1024,1024]{1,0:T(8,128)(2,1)}) %all-gather.14.cloned.1.call-update) | async-done | bytes 2097168 | tf_op jit(solution)/shard_map/all_gather | solution.py:104
  173.1 15.1 %scatter_custom_fusion = bf16[1408,1024]{1,0:T(8,128)(2,1)} fusion(s32[1024]{0:T(1024)} %get-tuple-element.150, bf16[128,1024]{1,0:T(8,128)(2,1)S(1)} %multiply_convert_fusion.3, s32[1024]{0:T(1024)S(1)} %broadcast_clamp_fusion, bf16[]{:T(256)} %constant.96.clone.1), kind=kCustom, calls=%fused_computation.133 | custom fusion | bytes 2884096
  205.8 51.1 %all-gather = bf16[16,64,32]{1,2,0:T(8,128)(2,1)S(1)} all-gather(bf16[1,64,32]{1,2,0:T(8,128)(2,1)S(1)} %bitcast.494), channel_id=1, replica_groups=mesh['rep'=8,'shard'=16] {'shard'}, dimensions={0}, use_global_device_ids=true | all-gather | bytes 69632 | tf_op jit(solution)/shard_map/all_gather | solution.py:105
  302.4 29.0 %all-to-all-done.4 = bf16[16,2,44,1024]{3,1,2,0:T(2,128)(2,1)} async-done(((bf16[16,2,44,1024]{3,1,2,0:T(2,128)(2,1)}), bf16[16,2,44,1024]{3,1,2,0:T(2,128)(2,1)}, u32[]{:S(2)}, u32[]{:S(2)}) %all-to-all-start.4) | async-done | bytes 2883616 | tf_op jit(solution)/shard_map/all_to_all | solution.py:210
  359.8 10.0 fusion.175
  397.5 9.3 fusion.100
  422.2 21.2 %gather_fusion = bf16[1024,1024]{1,0:T(8,128)(2,1)} fusion(bf16[32,44,1024]{2,0,1:T(8,128)(2,1)} %reshape.931, s32[1024]{0:T(1024)S(1)} %bitcast.421), kind=kCustom, calls=%fused_computation.1 | custom fusion | bytes 4202496 | tf_op jit(solution)/shard_map/gather | solution.py:188
  461.3 21.2 %gather_fusion.2 = bf16[1024,1024]{1,0:T(8,128)(2,1)} fusion(bf16[32,44,1024]{2,0,1:T(8,128)(2,1)} %reshape.943, s32[1024]{0:T(1024)S(1)} %bitcast.422), kind=kCustom, calls=%fused_computation.4 | custom fusion | bytes 4202496 | tf_op jit(solution)/shard_map/gather | solution.py:245
  487.3 14.7 %scatter_custom_fusion.1 = bf16[1408,1024]{1,0:T(8,128)(2,1)} fusion(s32[1024]{0:T(1024)} %get-tuple-element.149, bf16[128,1024]{1,0:T(8,128)(2,1)S(1)} %get-tuple-element.104, s32[1024]{0:T(1024)} %copy-done.116, bf16[]{:T(256)} %constant.96.clone.1), kind=kCustom, calls=%fused_computation.131 | custom fusion | bytes 2884096
  542.2 17.2 %all-to-all-done.2 = bf16[16,2,44,1024]{3,1,2,0:T(2,128)(2,1)} async-done(((bf16[16,2,44,1024]{3,1,2,0:T(2,128)(2,1)}), bf16[16,2,44,1024]{3,1,2,0:T(2,128)(2,1)}, u32[]{:S(2)}, u32[]{:S(2)}) %all-to-all-start.2) | async-done | bytes 2883616 | tf_op jit(solution)/shard_map/all_to_all | solution.py:177
  576.1 26.7 %all-to-all-done.6 = bf16[16,2,44,1024]{3,1,2,0:T(2,128)(2,1)} async-done(((bf16[16,2,44,1024]{3,1,2,0:T(2,128)(2,1)}), bf16[16,2,44,1024]{3,1,2,0:T(2,128)(2,1)}, u32[]{:S(2)}, u32[]{:S(2)}) %all-to-all-start.6) | async-done | bytes 2883616 | tf_op jit(solution)/shard_map/all_to_all | solution.py:210
  633.6 28.2 %all-to-all-done.3 = bf16[16,2,44,1024]{3,1,2,0:T(2,128)(2,1)} async-done(((bf16[16,2,44,1024]{3,1,2,0:T(2,128)(2,1)}), bf16[16,2,44,1024]{3,1,2,0:T(2,128)(2,1)}, u32[]{:S(2)}, u32[]{:S(2)}) %all-to-all-start.3) | async-done | bytes 2883616 | tf_op jit(solution)/shard_map/all_to_all | solution.py:183
  680.9 21.2 %gather_fusion.1 = bf16[1024,1024]{1,0:T(8,128)(2,1)} fusion(bf16[32,44,1024]{2,0,1:T(8,128)(2,1)} %reshape.941, s32[1024]{0:T(1024)S(1)} %bitcast.419), kind=kCustom, calls=%fused_computation.3 | custom fusion | bytes 4202496 | tf_op jit(solution)/shard_map/gather | solution.py:188
  719.9 21.3 %gather_fusion.3 = bf16[1024,1024]{1,0:T(8,128)(2,1)} fusion(bf16[32,44,1024]{2,0,1:T(8,128)(2,1)} %reshape.950, s32[1024]{0:T(1024)S(1)} %bitcast.420), kind=kCustom, calls=%fused_computation.5 | custom fusion | bytes 4202496 | tf_op jit(solution)/shard_map/gather | solution.py:245
  749.2 10.6 fusion.10
  759.9 10.9 fusion
  776.1 11.8 fusion.2
  809.6 10.5 fusion.12
  825.6 11.2 fusion.3
  836.8 12.2 fusion.5
  899.2 54.3 %reduce-scatter.8.cloned.1.call-done = f32[128,1024]{1,0:T(8,128)} async-done(((f32[2048,1024]{1,0:T(8,128)}), f32[128,1024]{1,0:T(8,128)}) %reduce-scatter.8.cloned.1.call-update) | async-done | bytes 524304 | tf_op jit(solution)/shard_map/reduce_scatter | solution.py:293
  1012.0 9.8 reduce-scatter.14.cloned.1.call-done
  1021.8 75.3 %reduce-scatter.12.cloned.1.call-done = f32[64,2048]{1,0:T(8,128)} async-done(((f32[1024,2048]{1,0:T(8,128)}), f32[64,2048]{1,0:T(8,128)}) %reduce-scatter.12.cloned.1.call-update) | async-done | bytes 524304 | tf_op jit(solution)/shard_map/reduce_scatter | solution.py:348
  1099.6 59.8 %reduce-scatter.16.cloned.1.call-done = f32[64,32]{1,0:T(8,128)} async-done(((f32[1024,32]{1,0:T(8,128)}), f32[64,32]{1,0:T(8,128)}) %reduce-scatter.16.cloned.1.call-update) | async-done | bytes 8208
  1166.7 32.9 %all-reduce.8 = (f32[1024]{0:T(1024)S(1)}, f32[1024]{0:T(1024)S(1)}, f32[64]{0:T(128)S(1)}, f32[64]{0:T(128)S(1)}) all-reduce(f32[1024]{0:T(1024)S(1)} %add.349, f32[1024]{0:T(1024)S(1)} %add.350, f32[64]{0:T(128)S(1)} %add.351, f32[64]{0:T(128)S(1)} %add.352), channel_id=7, replica_groups=mesh['rep'=8,'shard'=16] {'shard'}, use_global_device_ids=true, to_apply=%region_64.65.clone | all-reduce | flops 2176 | bytes 17408
  1199.9 40.5 %all-reduce.9 = (f32[64,32]{0,1:T(8,128)}, f32[64]{0:T(128)}, f32[64]{0:T(128)}, f32[4]{0:T(128)}, f32[4]{0:T(128)}) all-reduce(f32[64,32]{0,1:T(8,128)S(1)} %copy.399, f32[64]{0:T(128)S(1)} %dynamic-slice.5, f32[64]{0:T(128)S(1)} %dynamic-slice.7, f32[4]{0:T(128)S(1)} %dynamic-slice.9, ...), channel_id=1, replica_groups=mesh['rep'=8,'shard'=16] {'rep'}, use_global_device_ids=true, to_apply=%region_61.62 | all-reduce | flops 2184 | bytes 17472 | tf_op jit(solution)/shard_map/psum | solution.py:356
  1242.6 204.8 %all-reduce.14.cloned.1.call-done = (f32[64,2048]{1,0:T(8,128)}, f32[64,1024]{1,0:T(8,128)}, f32[2,1024,512]{2,1,0:T(8,128)}, f32[2,1024,512]{2,1,0:T(8,128)}, f32[2,512,1024]{2,1,0:T(8,128)}) async-done(((f32[64,2048]{1,0:T(8,128)}, f32[64,1024]{1,0:T(8,128)}, f32[2,1024,512]{2,1,0:T(8,128)}, f32[2,1024,512]{2,1,0:T(8,128)}, f32[2,512,1024]{2,1,0:T(8,128)}), (f32[64,2048]{1,0:T(8,128)}, ...) | async-done | bytes 13369360 | tf_op jit(solution)/shard_map/psum | solution.py:356
  (569 shorter events, 521.7 us)
Async XLA Ops:
  7.2 324.2 %copy-start = (bf16[2,512,1024]{2,1,0:T(8,128)(2,1)S(1)}, bf16[2,512,1024]{2,1,0:T(8,128)(2,1)}, u32[]{:S(2)}) copy-start(bf16[2,512,1024]{2,1,0:T(8,128)(2,1)} %param.29) | copy-start | bytes 6291460
  7.2 43.8 %all-gather.8.cloned.1.call-start = ((), (), s32[]{:S(2)}) async-start(), calls=%async_computation.13 | async-start | bytes 4456448 | tf_op jit(solution)/shard_map/all_gather | solution.py:103
  7.9 91.1 %all-gather.12.cloned.1.call-start = ((), (), s32[]{:S(2)}) async-start(), calls=%async_computation.15 | async-start | bytes 2228224 | tf_op jit(solution)/shard_map/all_gather | solution.py:138
  61.1 74.1 %all-gather.10.cloned.1.call-start = ((), (), s32[]{:S(2)}) async-start(), calls=%async_computation.14 | async-start | bytes 2228224 | tf_op jit(solution)/shard_map/all_gather | solution.py:139
  62.8 108.0 %all-gather.14.cloned.1.call-start = ((), (), s32[]{:S(2)}) async-start(), calls=%async_computation.16 | async-start | bytes 2228224 | tf_op jit(solution)/shard_map/all_gather | solution.py:104
  63.4 292.4 %all-gather.16.cloned.1.call-start = ((), (), s32[]{:S(2)}) async-start(), calls=%async_computation.17 | async-start | bytes 2228224 | tf_op jit(solution)/shard_map/all_gather | solution.py:139
  84.4 88.6 %copy-start.116 = (s32[1024]{0:T(1024)}, s32[1024]{0:T(1024)S(1)}, u32[]{:S(2)}) copy-start(s32[1024]{0:T(1024)S(1)} %broadcast_clamp_fusion) | copy-start | bytes 12292
  172.9 312.6 %copy-start.22 = (f32[128,1024]{1,0:T(8,128)}, f32[128,1024]{1,0:T(8,128)S(1)}, u32[]{:S(2)}) copy-start(f32[128,1024]{1,0:T(8,128)S(1)} %get-tuple-element.133) | copy-start | bytes 1572868
  173.1 87.7 %copy-start.39 = (bf16[128,1024]{1,0:T(8,128)(2,1)}, bf16[128,1024]{1,0:T(8,128)(2,1)S(1)}, u32[]{:S(2)}) copy-start(bf16[128,1024]{1,0:T(8,128)(2,1)S(1)} %multiply_convert_fusion.3) | copy-start | bytes 786436
  201.1 82.1 %all-to-all-start = ((bf16[16,2,44,1024]{3,1,2,0:T(2,128)(2,1)}), bf16[16,2,44,1024]{3,1,2,0:T(2,128)(2,1)}, u32[]{:S(2)}, u32[]{:S(2)}) async-start(bf16[16,2,44,1024]{3,1,2,0:T(2,128)(2,1)} %copy.299), calls=%async_computation | async-start | bytes 5767168 | tf_op jit(solution)/shard_map/all_to_all | solution.py:177
  283.2 48.2 %all-to-all-start.4 = ((bf16[16,2,44,1024]{3,1,2,0:T(2,128)(2,1)}), bf16[16,2,44,1024]{3,1,2,0:T(2,128)(2,1)}, u32[]{:S(2)}, u32[]{:S(2)}) async-start(bf16[16,2,44,1024]{3,1,2,0:T(2,128)(2,1)} %copy.320), calls=%async_computation.4 | async-start | bytes 5767168 | tf_op jit(solution)/shard_map/all_to_all | solution.py:210
  287.7 72.1 %all-gather.18.cloned.1.call-start = ((), (), s32[]{:S(2)}) async-start(), calls=%async_computation.18 | async-start | bytes 2228224 | tf_op jit(solution)/shard_map/all_gather | solution.py:138
  346.7 45.3 %all-to-all-start.1 = ((bf16[16,2,44,1024]{3,1,2,0:T(2,128)(2,1)}), bf16[16,2,44,1024]{3,1,2,0:T(2,128)(2,1)}, u32[]{:S(2)}, u32[]{:S(2)}) async-start(bf16[16,2,44,1024]{3,1,2,0:T(2,128)(2,1)} %copy.302), calls=%async_computation.1 | async-start | bytes 5767168 | tf_op jit(solution)/shard_map/all_to_all | solution.py:183
  392.0 55.6 %all-to-all-start.5 = ((bf16[16,2,44,1024]{3,1,2,0:T(2,128)(2,1)}), bf16[16,2,44,1024]{3,1,2,0:T(2,128)(2,1)}, u32[]{:S(2)}, u32[]{:S(2)}) async-start(bf16[16,2,44,1024]{3,1,2,0:T(2,128)(2,1)} %copy.322), calls=%async_computation.5 | async-start | bytes 5767168 | tf_op jit(solution)/shard_map/all_to_all | solution.py:241
  515.2 44.1 %all-to-all-start.2 = ((bf16[16,2,44,1024]{3,1,2,0:T(2,128)(2,1)}), bf16[16,2,44,1024]{3,1,2,0:T(2,128)(2,1)}, u32[]{:S(2)}, u32[]{:S(2)}) async-start(bf16[16,2,44,1024]{3,1,2,0:T(2,128)(2,1)} %copy.314), calls=%async_computation.2 | async-start | bytes 5767168 | tf_op jit(solution)/shard_map/all_to_all | solution.py:177
  559.3 43.5 %all-to-all-start.6 = ((bf16[16,2,44,1024]{3,1,2,0:T(2,128)(2,1)}), bf16[16,2,44,1024]{3,1,2,0:T(2,128)(2,1)}, u32[]{:S(2)}, u32[]{:S(2)}) async-start(bf16[16,2,44,1024]{3,1,2,0:T(2,128)(2,1)} %copy.342), calls=%async_computation.7 | async-start | bytes 5767168 | tf_op jit(solution)/shard_map/all_to_all | solution.py:210
  618.1 43.7 %all-to-all-start.3 = ((bf16[16,2,44,1024]{3,1,2,0:T(2,128)(2,1)}), bf16[16,2,44,1024]{3,1,2,0:T(2,128)(2,1)}, u32[]{:S(2)}, u32[]{:S(2)}) async-start(bf16[16,2,44,1024]{3,1,2,0:T(2,128)(2,1)} %copy.317), calls=%async_computation.3 | async-start | bytes 5767168 | tf_op jit(solution)/shard_map/all_to_all | solution.py:183
  661.8 44.5 %all-to-all-start.7 = ((bf16[16,2,44,1024]{3,1,2,0:T(2,128)(2,1)}), bf16[16,2,44,1024]{3,1,2,0:T(2,128)(2,1)}, u32[]{:S(2)}, u32[]{:S(2)}) async-start(bf16[16,2,44,1024]{3,1,2,0:T(2,128)(2,1)} %copy.344), calls=%async_computation.8 | async-start | bytes 5767168 | tf_op jit(solution)/shard_map/all_to_all | solution.py:241
  666.9 231.1 %reduce-scatter.10.cloned.1.call-start = ((), (), s32[]{:S(2)}) async-start(), calls=%async_computation.20 | async-start | bytes 8912896 | tf_op jit(solution)/shard_map/reduce_scatter | solution.py:293
  806.2 147.2 %reduce-scatter.8.cloned.1.call-start = ((), (), s32[]{:S(2)}) async-start(), calls=%async_computation.19 | async-start | bytes 8912896 | tf_op jit(solution)/shard_map/reduce_scatter | solution.py:293
  867.6 154.3 %reduce-scatter.14.cloned.1.call-start = ((), (), s32[]{:S(2)}) async-start(), calls=%async_computation.22 | async-start | bytes 4456448 | tf_op jit(solution)/shard_map/reduce_scatter | solution.py:349
  872.0 225.1 %reduce-scatter.12.cloned.1.call-start = ((), (), s32[]{:S(2)}) async-start(), calls=%async_computation.21 | async-start | bytes 8912896 | tf_op jit(solution)/shard_map/reduce_scatter | solution.py:348
  896.3 59.9 %copy-start.36 = (f32[128,512]{0,1:T(8,128)S(1)}, f32[128,512]{0,1:T(8,128)}, u32[]{:S(2)}) copy-start(f32[128,512]{0,1:T(8,128)} %copy-done.35) | copy-start | bytes 786436
  896.3 59.9 %copy-start.118 = (f32[64]{0:T(128)S(1)}, f32[64]{0:T(128)}, u32[]{:S(2)}) copy-start(f32[64]{0:T(128)} %copy-done.117) | copy-start | bytes 772
  974.8 184.5 %reduce-scatter.16.cloned.1.call-start = ((), (), s32[]{:S(2)}) async-start(), calls=%async_computation.23 | async-start | bytes 557056
  1003.9 443.5 %all-reduce.14.cloned.1.call-start = ((), (), s32[]{:S(2)}) async-start(), calls=%async_computation.24 | async-start | bytes 26738688 | tf_op jit(solution)/shard_map/psum | solution.py:356
  1097.1 63.1 %copy-start.104 = (f32[512]{0:T(512)S(1)}, f32[512]{0:T(512)}, u32[]{:S(2)}) copy-start(f32[512]{0:T(512)} %get-tuple-element.70) | copy-start | bytes 6148
  1097.1 63.2 %copy-start.105 = (f32[512]{0:T(512)S(1)}, f32[512]{0:T(512)}, u32[]{:S(2)}) copy-start(f32[512]{0:T(512)} %get-tuple-element.68) | copy-start | bytes 6148
  1098.7 65.5 %copy-start.57 = (bf16[128,1024]{1,0:T(8,128)(2,1)S(1)}, bf16[128,1024]{1,0:T(8,128)(2,1)}, u32[]{:S(2)}) copy-start(bf16[128,1024]{1,0:T(8,128)(2,1)} %get-tuple-element.67) | copy-start | bytes 786436
  1098.7 65.5 %copy-start.66 = (bf16[128,512]{1,0:T(8,128)(2,1)S(1)}, bf16[128,512]{1,0:T(8,128)(2,1)}, u32[]{:S(2)}) copy-start(bf16[128,512]{1,0:T(8,128)(2,1)} %copy-done.65) | copy-start | bytes 393220
  1098.7 65.5 %copy-start.103 = (f32[128]{0:T(128)S(1)}, f32[128]{0:T(128)}, u32[]{:S(2)}) copy-start(f32[128]{0:T(128)} %copy-done.102) | copy-start | bytes 1540
  1164.3 76.1 %copy-start.112 = (f32[128]{0:T(128)S(1)}, f32[128]{0:T(128)}, u32[]{:S(2)}) copy-start(f32[128]{0:T(128)} %copy-done.110) | copy-start | bytes 1540
  (118 other events, 1141.4 us)
Sparse Core Ops, SparseCore 0:
  9.7 41.1 all-gather.7
  61.2 37.5 all-gather.11
  101.1 34.0 all-gather.9
  136.7 34.0 all-gather.13
  172.3 33.9 all-gather.15
  290.4 53.5 all-gather.17
  806.3 71.4 reduce-scatter.9
  880.2 73.1 reduce-scatter.7
  956.4 65.3 reduce-scatter.13
  1024.1 72.9 reduce-scatter.11
  1100.0 59.2 reduce-scatter.15
  1163.0 284.3 all-reduce.13
where the time goes:
time: 1480 us; the launch traced here: 1470 us
  waiting for transfers between devices  553 us (37%)
  local copies, waits for them, and re-layouts  338 us (23%)
  matrix products  221 us (15%)
  blocking collectives  154 us (10%)
  other arithmetic  139 us (9%)
  starting transfers between devices  45.4 us (3%)
  between operations  19 us (1%)
    psum x1, waiting for transfers between devices, local(): lax.psum((owned[0], owned[1], owned[2], owned[3], owned[4], owned[5], own...  205 us
    reduce_scatter x1, waiting for transfers between devices, local(): lax.psum_scatter(front_totals[0], 'shard', scatter_dimension=0, tiled=True)  75.3 us
    unnamed x2, blocking collectives  62 us
    unnamed x13, waiting for transfers between devices  61.1 us
    unnamed x283, local copies, waits for them, and re-layouts  60.4 us
    all_to_all x2, waiting for transfers between devices, local(): lax.all_to_all(grad_dispatch.reshape(shards, local_experts, capacity, D),...  55.7 us
    reduce_scatter x2, waiting for transfers between devices, local(): lax.psum_scatter(jnp.concatenate([key_grad.reshape(lax.axis_size('shard')...  54.3 us
    all_gather x1, blocking collectives, local(): lax.all_gather(w_router, 'shard', axis=0, tiled=True)  51.1 us
  transfers between devices with their start and end apart: 20, of which 13 were waited for; matrix products, arithmetic and copies ran while one was open for 33% of the time, Pallas kernels for 0%

commit v1 on v0

v1 whole, which is shorter than its diff:
```python
import functools

import jax
import jax.numpy as jnp
from jax import lax
from jax.experimental import pallas as pl
from jax.experimental.pallas import tpu as pltpu
from jax.sharding import PartitionSpec as P

D = 1024
HEADS = 16
KV_HEADS = 8
HD = 64
HALF = HD // 2
FF = 512
TOP = 8
MICRO = 2
SEQS = 8
SHARDS = 16
REPS = 8
CHIPS = 8
TPD = 128
G = SHARDS * TPD
EXPERTS = 32
LOCAL_EXPERTS = EXPERTS // SHARDS
SLOTS = 48
ROWS = SHARDS * SLOTS
PART = 4
PARTS = SHARDS // PART
CHUNK = 256
CHUNKS = G // CHUNK
HEAD_COLS = 3 * HD
PACK = 256
APART = 256.0
EPS = 1e-06

F32 = jnp.float32
BF16 = jnp.bfloat16
MIB = 1 << 20

BRIEF = pl.CostEstimate(flops=1_000_000, bytes_accessed=1_000_000, transcendentals=0)

SAME_CORE = [[core + 2 * chip for chip in range(CHIPS)] for core in range(2)]
OTHER_CORE = [(index, index ^ 1) for index in range(SHARDS)]


def mm(a, b, left, right):
    return lax.dot_general(a, b, (((left,), (right,)), ((), ())), preferred_element_type=F32)


def rms_scale(values, axis=-1):
    return lax.rsqrt(jnp.mean(values * values, axis=axis, keepdims=True) + EPS)


def norm_back(grad_hat, normed, scale, axis=-1):
    return scale * (grad_hat - normed * jnp.mean(grad_hat * normed, axis=axis, keepdims=True))


def turn(values, cosine, sine):
    first, second = values[:HALF], values[HALF:]
    return jnp.concatenate(
        [first * cosine - second * sine, second * cosine + first * sine], axis=0
    )


def attn_fwd_kernel(
    x_ref,
    w_ref,
    ga_ref,
    gq_ref,
    gk_ref,
    tab_ref,
    ain_ref,
    raw_ref,
    key_ref,
    keyt_ref,
    val_ref,
    query_ref,
    out_ref,
    outf_ref,
    inv_ref,
    valt,
):
    step = pl.program_id(1)
    x = x_ref[...].reshape(CHUNK, D).astype(F32)
    attn_in = (x * rms_scale(x) * ga_ref[...]).astype(BF16)
    ain_ref[0] = attn_in
    raw = mm(w_ref[...], attn_in, 1, 1)
    raw_ref[0, step] = raw[: 2 * HD]
    table = tab_ref[0, step]
    cosine, sine = table[:HALF], table[HALF:HD]
    far, own = table[HD : HD + SEQS], table[HD + SEQS :]
    query_raw, key_raw, value = raw[:HD], raw[HD : 2 * HD], raw[2 * HD :]
    query = turn(query_raw * rms_scale(query_raw, 0) * gq_ref[...], cosine, sine).astype(BF16)
    key = turn(key_raw * rms_scale(key_raw, 0) * gk_ref[...], cosine, sine).astype(BF16)
    pad = jnp.zeros((HD - SEQS, CHUNK), F32)
    query_ref[0, step] = jnp.concatenate(
        [query.astype(F32) * HD**-0.5, far, pad], axis=0
    ).astype(BF16)
    keyt_ref[0, step] = key
    key_rows = jnp.concatenate([key.astype(F32), own, pad], axis=0)
    key_ref[0, pl.ds(step * CHUNK, CHUNK), :] = key_rows.T.astype(BF16)
    place = lax.broadcasted_iota(jnp.int32, (HD, CHUNK), 0)
    val_rows = jnp.concatenate([value, (place < 2).astype(F32)], axis=0)
    val_ref[0, pl.ds(step * CHUNK, CHUNK), :] = val_rows.T.astype(BF16)
    valt[:, pl.ds(pl.multiple_of(step * CHUNK, CHUNK), CHUNK)] = val_rows[: HD + 16].astype(BF16)

    @pl.when(step == CHUNKS - 1)
    def attend():
        tokens = pl.ds(pl.multiple_of(pl.program_id(0) * TPD, TPD), TPD)

        def one(j, carry):
            weights = jnp.exp(mm(key_ref[0], query_ref[0, j], 1, 0)).astype(BF16)
            total = mm(valt[...], weights, 1, 0)
            inv = 1.0 / total[HD : HD + 1]
            attended = total[:HD] * inv
            inv_ref[0, j] = inv
            outf_ref[0, j] = attended
            low = attended.astype(BF16)
            out_ref[2 * j, :, tokens] = low[:, :TPD]
            out_ref[2 * j + 1, :, tokens] = low[:, TPD:]
            return carry

        lax.fori_loop(0, CHUNKS, one, 0)


def attn_fwd(x_all, w_head, attn_gain, query_gain, key_gain, tables):
    whole = lambda *shape: pl.BlockSpec(shape, lambda m, i: (0,) * len(shape))
    each = lambda *shape: pl.BlockSpec((1, *shape), lambda m, i: (m,) + (0,) * len(shape))
    shapes = (
        ((MICRO, G, D), BF16),
        ((MICRO, CHUNKS, 2 * HD, CHUNK), F32),
        ((MICRO, G, 2 * HD), BF16),
        ((MICRO, CHUNKS, HD, CHUNK), BF16),
        ((MICRO, G, 2 * HD), BF16),
        ((MICRO, CHUNKS, 2 * HD, CHUNK), BF16),
        ((SHARDS, HD, MICRO * TPD), BF16),
        ((MICRO, CHUNKS, HD, CHUNK), F32),
        ((MICRO, CHUNKS, 1, CHUNK), F32),
    )
    return pl.pallas_call(
        attn_fwd_kernel,
        grid=(MICRO, CHUNKS),
        in_specs=[
            pl.BlockSpec((CHUNK // TPD, TPD, D), lambda m, i: (i, m, 0)),
            whole(HEAD_COLS, D),
            whole(1, D),
            whole(HD, 1),
            whole(HD, 1),
            each(CHUNKS, HD + 2 * SEQS, CHUNK),
        ],
        out_specs=[
            pl.BlockSpec((1, CHUNK, D), lambda m, i: (m, i, 0)),
        ]
        + [each(*shape[1:]) for shape, _ in shapes[1:6]]
        + [whole(*shapes[6][0])]
        + [each(*shape[1:]) for shape, _ in shapes[7:]],
        out_shape=[jax.ShapeDtypeStruct(shape, dtype) for shape, dtype in shapes],
        scratch_shapes=[pltpu.VMEM((HD + 16, G), BF16)],
        compiler_params=pltpu.CompilerParams(vmem_limit_bytes=60 * MIB),
        cost_estimate=BRIEF,
        name="attn_fwd",
    )(x_all, w_head, attn_gain, query_gain, key_gain, tables)


def attn_bwd_kernel(
    grad_ref,
    outf_ref,
    inv_ref,
    key_ref,
    keyt_ref,
    val_ref,
    query_ref,
    raw_ref,
    ain_ref,
    gq_ref,
    gk_ref,
    tab_ref,
    dproj_ref,
    gw_ref,
    gain_ref,
    dq_s,
    dk_s,
    dv_s,
):
    keyt = jnp.concatenate([keyt_ref[0, j] for j in range(CHUNKS)], axis=1)
    dk_s[...] = jnp.zeros_like(dk_s)
    dv_s[...] = jnp.zeros_like(dv_s)
    pad = jnp.zeros((HD - 2, CHUNK), F32)

    def one(j, carry):
        grad = jnp.concatenate([grad_ref[2 * j], grad_ref[2 * j + 1]], axis=1).astype(F32)
        grad = grad * inv_ref[0, j]
        low = grad.astype(BF16)
        dot = -jnp.sum(low.astype(F32) * outf_ref[0, j], axis=0, keepdims=True)
        dot_high = dot.astype(BF16).astype(F32)
        rows = jnp.concatenate([grad, dot_high, dot - dot_high, pad], axis=0)
        query = query_ref[0, j]
        weights = jnp.exp(mm(key_ref[0], query, 1, 0))
        centred = mm(val_ref[0], rows.astype(BF16), 1, 0)
        dscores = (weights * centred).astype(BF16)
        dq_s[j] = mm(keyt, dscores, 1, 0) * HD**-0.5
        dk_s[...] += mm(dscores, query.astype(F32).T.astype(BF16), 1, 0)
        dv_s[...] += mm(weights.astype(BF16), rows.T.astype(BF16), 1, 0)
        return carry

    lax.fori_loop(0, CHUNKS, one, 0)
    gq, gk = gq_ref[...], gk_ref[...]
    gw_ref[...] = jnp.zeros_like(gw_ref)
    gain_ref[...] = jnp.zeros_like(gain_ref)

    def back(j, carry):
        tokens = pl.ds(j * CHUNK, CHUNK)
        cosine, sine = tab_ref[0, j, :HALF], -tab_ref[0, j, HALF:HD]
        raw = raw_ref[0, j]
        dk = dk_s[tokens, :].T[:HD]
        dv = dv_s[tokens, :].T[:HD]
        parts = []
        gains = []
        for grad, values, gain in ((dq_s[j], raw[:HD], gq), (dk, raw[HD:], gk)):
            normed_grad = turn(grad, cosine, sine)
            scale = rms_scale(values, 0)
            hat = values * scale
            gains.append(jnp.sum(normed_grad * hat, axis=1, keepdims=True))
            parts.append(norm_back(normed_grad * gain, hat, scale, 0))
        dproj = jnp.concatenate(parts + [dv], axis=0).astype(BF16)
        dproj_ref[2 * j] = dproj[:, :TPD]
        dproj_ref[2 * j + 1] = dproj[:, TPD:]
        gw_ref[...] += mm(dproj, ain_ref[0, tokens, :], 1, 0)
        gain_ref[...] += jnp.concatenate(
            [jnp.broadcast_to(g, (HD, TPD)) for g in gains], axis=0
        )
        return carry

    lax.fori_loop(0, CHUNKS, back, 0)


def attn_bwd(m, grad, *operands):
    shapes = (
        ((SHARDS, HEAD_COLS, TPD), BF16),
        ((HEAD_COLS, D), F32),
        ((2 * HD, TPD), F32),
    )
    whole = lambda *shape: pl.BlockSpec(shape, lambda i: (0,) * len(shape))
    each = lambda *shape: pl.BlockSpec((1, *shape), lambda i: (m,) + (0,) * len(shape))
    return pl.pallas_call(
        attn_bwd_kernel,
        grid=(1,),
        in_specs=[whole(*grad.shape)]
        + [each(*v.shape[1:]) if v.shape[0] == MICRO else whole(*v.shape) for v in operands],
        out_specs=[whole(*shape) for shape, _ in shapes],
        out_shape=[jax.ShapeDtypeStruct(shape, dtype) for shape, dtype in shapes],
        scratch_shapes=[
            pltpu.VMEM((CHUNKS, HD, CHUNK), F32),
            pltpu.VMEM((G, 2 * HD), F32),
            pltpu.VMEM((G, 2 * HD), F32),
        ],
        compiler_params=pltpu.CompilerParams(vmem_limit_bytes=60 * MIB),
        cost_estimate=BRIEF,
        name="attn_bwd",
    )(grad, *operands)


def expert_kernel(core_ref, *refs, later, kinds, waits):
    refs = refs[waits:]
    rows_refs, refs = refs[: kinds[0]], refs[kinds[0] :]
    grads_refs, refs = refs[: kinds[1]], refs[kinds[1] :]
    slot_ref, gate_ref, wg_ref, wu_ref, wd_ref, *refs = refs
    before_refs = (None,) * 3
    if later:
        before_refs = (refs[2], refs[0], refs[1])
        refs = refs[3:]
    out_refs, back_refs = refs[:2], refs[2:4]
    route_ref, gg_ref, gu_ref, gd_ref = refs[4:8]
    xs, cs, ps, ys, ds = refs[8:]
    step = pl.program_id(0)
    slots = lax.broadcasted_iota(jnp.int32, (SLOTS, TPD), 0).astype(F32)

    def block(refs, k):
        if len(refs) == 2:
            return refs[k % 2][k // 2]
        return refs[0][k ^ core_ref[0]]

    def hot_of(expert, source):
        return slots == slot_ref[expert, pl.ds(source, 1), :]

    @pl.when(step < PARTS)
    def pick():
        for k in range(PART):
            source = step * PART + k
            hots = [hot_of(e, source) for e in range(LOCAL_EXPERTS)]
            low = jnp.concatenate(hots, axis=0).astype(BF16)
            shape = (LOCAL_EXPERTS, SLOTS, D)
            xs[:, source] = mm(low, block(rows_refs, k), 1, 0).astype(BF16).reshape(shape)
            cs[:, source] = mm(low, block(grads_refs, k), 1, 0).astype(BF16).reshape(shape)
            for e in range(LOCAL_EXPERTS):
                gate = jnp.where(hots[e], gate_ref[e, pl.ds(source, 1), :], 0.0)
                ps[e, source] = jnp.broadcast_to(
                    jnp.sum(gate, axis=1, keepdims=True), (SLOTS, TPD)
                )

    @pl.when((step >= PARTS) & (step < PARTS + LOCAL_EXPERTS))
    def work():
        expert = step - PARTS
        w_gate, w_up, w_down = wg_ref[0], wu_ref[0], wd_ref[0]
        x = xs[expert].reshape(ROWS, D)
        c = cs[expert].reshape(ROWS, D).astype(F32)
        prob = ps[expert].reshape(ROWS, TPD)[:, :1]
        gate = mm(x, w_gate, 1, 0)
        up = mm(x, w_up, 1, 0)
        sigmoid = 1.0 / (1.0 + jnp.exp(-gate))
        active = gate * sigmoid
        hidden = (active * up).astype(BF16)
        made = mm(hidden, w_down, 1, 0).astype(BF16).astype(F32)
        ys[:, expert] = (made * prob).astype(BF16).reshape(SHARDS, SLOTS, D)
        ps[expert] = jnp.broadcast_to(
            jnp.sum(made * c, axis=1, keepdims=True), (ROWS, TPD)
        ).reshape(SHARDS, SLOTS, TPD)
        dmade = (prob * c).astype(BF16)
        dhidden = mm(dmade, w_down, 1, 1)
        dgate = (dhidden * up * (sigmoid + active * (1.0 - sigmoid))).astype(BF16)
        dup = (dhidden * active).astype(BF16)
        drows = mm(dgate, w_gate, 1, 1) + mm(dup, w_up, 1, 1)
        ds[:, expert] = drows.astype(BF16).reshape(SHARDS, SLOTS, D)
        for total_ref, before, left, right in zip(
            (gd_ref, gg_ref, gu_ref), before_refs, (hidden, x, x), (dmade, dgate, dup)
        ):
            term = mm(left, right, 0, 0)
            if later:
                term = term + before[0].astype(F32)
            total_ref[0] = term.astype(BF16)

    @pl.when(step >= PARTS + LOCAL_EXPERTS)
    def put():
        for k in range(PART):
            source = (step - PARTS - LOCAL_EXPERTS) * PART + k
            hots = [hot_of(e, source) for e in range(LOCAL_EXPERTS)]
            low = jnp.concatenate(hots, axis=0).astype(BF16)
            back_refs[k % 2][k // 2] = mm(low, ds[source].reshape(-1, D), 0, 0).astype(BF16)
            out_refs[k % 2][k // 2] = mm(low, ys[source].reshape(-1, D), 0, 0).astype(BF16)
            for e in range(LOCAL_EXPERTS):
                route_ref[e, pl.ds(source, 1), :] = jnp.sum(
                    jnp.where(hots[e], ps[e, source], 0.0), axis=0, keepdims=True
                )


def experts_step(waits, m, core, rows, grads, slot, gate, w_gate, w_up, w_down, previous):
    later = previous is not None
    whole = lambda *shape: pl.BlockSpec(shape, lambda i, at: (0,) * len(shape))
    first = lambda i, at: (jnp.minimum(i, PARTS - 1), 0, 0)
    kinds = (len(rows), 1)
    of_micro = lambda i, at: (jnp.minimum(i, PARTS - 1), m, 0)
    last = lambda i, at: (jnp.maximum(i - PARTS - LOCAL_EXPERTS, 0), 0, 0)
    each = lambda *shape: pl.BlockSpec(
        (1, *shape), lambda i, at: (jnp.clip(i - PARTS, 0, LOCAL_EXPERTS - 1), 0, 0)
    )
    weight_specs = [each(D, FF), each(D, FF), each(FF, D)]
    shapes = [
        *[((CHIPS, TPD, D), BF16)] * 4,
        ((LOCAL_EXPERTS, SHARDS, TPD), F32),
        (w_gate.shape, BF16),
        (w_up.shape, BF16),
        (w_down.shape, BF16),
    ]
    return pl.pallas_call(
        functools.partial(expert_kernel, later=later, kinds=kinds, waits=len(waits)),
        grid_spec=pltpu.PrefetchScalarGridSpec(
            num_scalar_prefetch=1,
            grid=(2 * PARTS + LOCAL_EXPERTS,),
            in_specs=[
                *[pl.BlockSpec(memory_space=pl.ANY)] * len(waits),
                *[pl.BlockSpec((PART // len(rows), TPD, D), first)] * len(rows),
                pl.BlockSpec((PART, TPD, D), of_micro),
            whole(LOCAL_EXPERTS, SHARDS, TPD),
            whole(LOCAL_EXPERTS, SHARDS, TPD),
        ]
        + weight_specs
        + (weight_specs if later else []),
        out_specs=[
            *[pl.BlockSpec((PART // 2, TPD, D), last)] * 4,
            whole(LOCAL_EXPERTS, SHARDS, TPD),
        ]
        + weight_specs,
        scratch_shapes=[
            pltpu.VMEM((LOCAL_EXPERTS, SHARDS, SLOTS, D), BF16),
            pltpu.VMEM((LOCAL_EXPERTS, SHARDS, SLOTS, D), BF16),
            pltpu.VMEM((LOCAL_EXPERTS, SHARDS, SLOTS, TPD), F32),
            pltpu.VMEM((SHARDS, LOCAL_EXPERTS, SLOTS, D), BF16),
            pltpu.VMEM((SHARDS, LOCAL_EXPERTS, SLOTS, D), BF16),
        ],
        ),
        out_shape=[jax.ShapeDtypeStruct(shape, dtype) for shape, dtype in shapes],
        compiler_params=pltpu.CompilerParams(vmem_limit_bytes=60 * MIB),
        cost_estimate=BRIEF,
        name="experts",
    )(core, *waits, *rows, grads, slot, gate, w_gate, w_up, w_down, *(previous if later else ()))


def gather(values):
    return lax.all_gather(values, "shard", axis=0)


def nothing(values_ref, earlier_ref, out_ref):
    del values_ref, earlier_ref, out_ref


def after(values, earlier):
    anywhere = pl.BlockSpec(memory_space=pl.ANY)
    return pl.pallas_call(
        nothing,
        in_specs=[anywhere] * 2,
        out_specs=anywhere,
        out_shape=jax.ShapeDtypeStruct(values.shape, values.dtype),
        input_output_aliases={0: 0},
        cost_estimate=BRIEF,
        name="after",
    )(values, earlier)


Y_SWAP = [(index, (index + 8) % SHARDS) for index in range(SHARDS)]
X_SHIFTS = [
    [(index, index // 8 * 8 + (index + 2 * shift) % 8) for index in range(SHARDS)]
    for shift in range(1, 4)
]


def permute(values, pairs):
    return lax.ppermute(values, "shard", pairs)


def gather_cores(values):
    like = exchange(
        jnp.broadcast_to(values[None], (CHIPS, *values.shape)), groups=SAME_CORE
    )
    return like, permute(like, OTHER_CORE)


def exchange(values, axis="shard", groups=None):
    return lax.all_to_all(
        values, axis, split_axis=0, concat_axis=0, tiled=True, axis_index_groups=groups
    )


def sum_cores(keep, give):
    return (keep.astype(F32) + permute(give, OTHER_CORE).astype(F32)).astype(BF16)


def sum_by_permutes(keep, give, shard):
    x, y = shard % 8 // 2, shard // 8
    chip = sum_cores(keep, give).reshape(2, 4, *keep.shape[1:])
    column = lambda k: lax.dynamic_index_in_dim(chip, (x + k) % 4, 1, keepdims=False)
    total = column(0).astype(F32)
    for k, shift in enumerate(X_SHIFTS):
        total = total + permute(column(k + 1), shift).astype(F32)
    row = lambda k: lax.dynamic_index_in_dim(total, k, 0, keepdims=False)
    return row(y) + permute(row(1 - y).astype(BF16), Y_SWAP).astype(F32)


def routed_softmax(logits, hits):
    top = jnp.max(jnp.where(hits, logits, -jnp.inf), axis=0, keepdims=True)
    powers = jnp.where(hits, jnp.exp(jnp.where(hits, logits - top, 0.0)), 0.0)
    return powers / jnp.sum(powers, axis=0, keepdims=True)


def local(
    block_input,
    cotangent,
    routes,
    lengths,
    stream_slot,
    w_qkv,
    w_out,
    w_router,
    g_attn,
    g_moe,
    g_q,
    g_k,
    w_gate,
    w_up,
    w_down,
):
    shard = lax.axis_index("shard")
    core = shard % 2
    q_width = HEADS * HD
    kv_width = KV_HEADS * HD
    own_rows = D // SHARDS
    micro = lambda values, m: values[m * TPD : (m + 1) * TPD]

    x_all = gather(block_input)

    doubled = lambda part: jnp.repeat(part.reshape(own_rows, KV_HEADS, HD), 2, axis=1)
    column = lambda v: jnp.pad(v, (0, own_rows - v.shape[0]))[:, None]
    small = jnp.concatenate([w_router, column(g_attn), column(g_moe), column(g_q), column(g_k)], 1)
    small = jnp.pad(small, ((0, 0), (0, PACK - HEAD_COLS - small.shape[1])))
    packed = jnp.concatenate(
        [
            w_qkv[:, :q_width].reshape(own_rows, HEADS, HD),
            doubled(w_qkv[:, q_width : q_width + kv_width]),
            doubled(w_qkv[:, q_width + kv_width :]),
            jnp.broadcast_to(small[:, None], (own_rows, SHARDS, PACK - HEAD_COLS)),
        ],
        axis=2,
    )
    packed = exchange(packed.transpose(1, 0, 2))
    flat = packed.reshape(D, PACK)
    w_head = flat[:, :HEAD_COLS].T
    rest = flat[:, HEAD_COLS:].astype(F32)
    router = flat[:, HEAD_COLS : HEAD_COLS + EXPERTS]
    attn_gain = rest[:, EXPERTS][None]
    moe_gain = rest[:, EXPERTS + 1][None]
    quarter = rest.reshape(SHARDS, own_rows, -1)[:, : HD // SHARDS]
    query_gain = quarter[:, :, EXPERTS + 2].reshape(HD, 1)
    key_gain = quarter[:, :, EXPERTS + 3].reshape(HD, 1)

    freq = 10000.0 ** (-2.0 * jnp.arange(HALF, dtype=F32) / HD)
    earlier = jnp.triu(jnp.ones((TPD, TPD), BF16), 1)

    hits = []
    for m in range(MICRO):
        named = micro(routes, m).T
        hits.append(jnp.any(named[None] == jnp.arange(EXPERTS)[:, None, None], axis=1))
    extra = jnp.stack(hits).astype(BF16).reshape(MICRO * 4, D)
    extra = jnp.pad(extra, ((0, 16 - MICRO * 4), (0, 0)))
    ordered = jnp.arange(SHARDS) ^ core
    ends = jnp.cumsum(lengths[0], axis=1)
    stream = stream_slot[0][:, None, :]
    past = (stream >= ends[:, :, None]).astype(jnp.int32)
    seq_id = jnp.sum(past, axis=1, keepdims=True)
    position = stream - jnp.sum(past * lengths[0][:, :, None], axis=1, keepdims=True)
    angle = freq[:, None] * position.astype(F32)
    own = (seq_id == jnp.arange(SEQS)[:, None]).astype(F32)
    tables = jnp.concatenate([jnp.cos(angle), jnp.sin(angle), (own - 1.0) * APART, own], axis=1)
    tables = tables.reshape(MICRO, -1, CHUNKS, CHUNK).transpose(0, 2, 1, 3)
    for ready in (flat, tables):
        x_all = after(x_all, ready)
    grads_all = gather(after(jnp.concatenate([cotangent, extra, w_out], axis=0), x_all))
    hits_all = grads_all[:, MICRO * TPD : MICRO * TPD + 16]
    hits_all = hits_all.reshape(SHARDS, 2 * MICRO, EXPERTS, TPD)[ordered]
    out_full = grads_all[:, MICRO * TPD + 16 :].reshape(q_width, D)
    attn_in_all, raw, key, keyt, val, query, out, outf, inv = attn_fwd(
        x_all, w_head, attn_gain, query_gain, key_gain, tables
    )
    attended = after(exchange(out), grads_all).reshape(q_width, MICRO * TPD)
    x = block_input.astype(F32)
    mid = x + mm(attended, out_full, 0, 0)
    moe_scale = rms_scale(mid)
    moe_hat = mid * moe_scale
    moe_in = (moe_hat * moe_gain).astype(BF16)
    rows_all = [gather_cores(micro(moe_in, 0)), (gather(micro(moe_in, 1)),)]

    experts_own = shard * LOCAL_EXPERTS
    grads, sums, chips = None, [], []
    for m in range(MICRO):
        hit = hits_all[:, m]
        before = jnp.einsum("set,tu->seu", hit, earlier, preferred_element_type=F32)
        slot = jnp.where(hit > 0, before, -1.0)
        slot = lax.dynamic_slice_in_dim(slot, experts_own, LOCAL_EXPERTS, 1).transpose(1, 0, 2)
        if m == 1:
            logits = mm(router, rows_all[1][0].reshape(G, D), 0, 1)
            logits = logits.reshape(EXPERTS, SHARDS, TPD)[:, ordered].reshape(EXPERTS, G)
        else:
            logits = jnp.stack(
                [mm(router, rows.reshape(G // 2, D), 0, 1) for rows in rows_all[m]], axis=1
            ).reshape(EXPERTS, 2, CHIPS, TPD)
            logits = logits.transpose(0, 2, 1, 3).reshape(EXPERTS, G)
        gate = routed_softmax(logits, hit.transpose(1, 0, 2).reshape(EXPERTS, G) > 0)
        gate = lax.dynamic_slice_in_dim(gate, experts_own, LOCAL_EXPERTS, 0)
        *parts, route, g_gate, g_up, g_down = experts_step(
            (chips[0],) if m else (),
            m,
            core.reshape(1),
            rows_all[m],
            grads_all,
            slot,
            gate.reshape(LOCAL_EXPERTS, SHARDS, TPD),
            w_gate,
            w_up,
            w_down,
            grads,
        )
        grads = (g_gate, g_up, g_down)
        sums.append((parts[:2], route))
        if m == 0:
            chips.append(sum_cores(*parts[2:]))
            qkv_full = lax.all_gather(after(w_qkv, route), "shard", axis=0, tiled=True)
    grad_experts = lax.psum(tuple(grads), "rep")

    out_part = jnp.zeros((q_width, D), F32)
    small_part = jnp.zeros((D, EXPERTS + 1), F32)
    grad_mid, grad_attended, back_attn = [], [], []
    for m in range(MICRO):
        route = sums[m][1]
        scale, hat, rows_in = (micro(v, m) for v in (moe_scale, moe_hat, moe_in))
        route_grad = exchange(route.transpose(1, 0, 2)[ordered]).reshape(EXPERTS, TPD)
        came = exchange(chips[m], groups=SAME_CORE)
        if m:
            came = after(came, back_attn[0][0])
        dmoe_in = jnp.sum(came.astype(F32), axis=0)
        gate = routed_softmax(mm(router, rows_in, 0, 1), hits[m])
        dlogits = gate * (route_grad - jnp.sum(gate * route_grad, axis=0, keepdims=True))
        dlogits = dlogits.astype(BF16)
        dmoe_in = dmoe_in + mm(dlogits, router, 0, 1)
        moe_part = jnp.sum(dmoe_in * hat, axis=0)
        small_part = small_part + jnp.concatenate(
            [mm(rows_in, dlogits, 0, 1), moe_part[:, None]], axis=1
        )
        dmid = micro(cotangent, m).astype(F32) + norm_back(dmoe_in * moe_gain, hat, scale)
        low = dmid.astype(BF16)
        out_part = out_part + mm(attended[:, m * TPD : (m + 1) * TPD], low, 1, 0)
        dattended = mm(out_full, low, 1, 1).astype(BF16)
        grad_mid.append(dmid)
        grad_attended.append(exchange(dattended.reshape(SHARDS, HD, TPD)))
        if m == 0:
            chips.append(sum_cores(after(parts[2], grad_attended[0]), parts[3]))
            grad_attended[0] = after(grad_attended[0], chips[1])
        back_attn.append(
            attn_bwd(
                m,
                grad_attended[m],
                outf,
                inv,
                key,
                keyt,
                val,
                query,
                raw,
                attn_in_all,
                query_gain,
                key_gain,
                tables,
            )
        )
    blocks = out_part.astype(BF16).reshape(CHIPS, 2, own_rows, D)
    out_own = sum_by_permutes(
        lax.dynamic_index_in_dim(blocks, core, 1, keepdims=False),
        lax.dynamic_index_in_dim(blocks, 1 - core, 1, keepdims=False),
        shard,
    )

    outputs = []
    for m in range(MICRO):
        keep, give = sums[m][0]
        total = sum_by_permutes(keep, after(give, grad_attended[1]), shard)
        outputs.append((micro(mid, m) + total).astype(BF16))

    input_grads = []
    attn_part = jnp.zeros((D,), F32)
    head_part = jnp.zeros((HEAD_COLS, D), F32)
    gain_part = jnp.zeros((2 * HD,), F32)
    for m in range(MICRO):
        dproj, head_grad, gains = back_attn[m]
        head_part = head_part + head_grad
        gain_part = gain_part + gains[:, 0]
        dproj = exchange(dproj if m else after(dproj, grad_attended[1]))
        paired = dproj[:, HD:].astype(F32).reshape(KV_HEADS, 2, 2, HD, TPD).sum(axis=1)
        dproj = jnp.concatenate(
            [
                dproj[:, :HD].reshape(q_width, TPD),
                paired[:, 0].reshape(kv_width, TPD).astype(BF16),
                paired[:, 1].reshape(kv_width, TPD).astype(BF16),
            ],
            axis=0,
        )
        here = micro(x, m)
        scale = rms_scale(here)
        hat = here * scale
        dattn_in = mm(dproj, qkv_full, 0, 1)
        attn_part = attn_part + jnp.sum(dattn_in * hat, axis=0)
        dx = grad_mid[m] + norm_back(dattn_in * attn_gain, hat, scale)
        input_grads.append(dx.astype(BF16))

    fours = gain_part.reshape(2, SHARDS, HD // SHARDS).transpose(1, 2, 0)
    fours = jnp.pad(fours, ((0, 0), (0, own_rows - HD // SHARDS), (0, 0))).reshape(D, 2)
    packed = jnp.concatenate([head_part.T, small_part, attn_part[:, None], fours], axis=1)
    packed = jnp.pad(packed, ((0, 0), (0, PACK - packed.shape[1]))).astype(BF16)
    for output in outputs:
        packed = after(packed, output)
    got = exchange(packed.reshape(SHARDS, own_rows, PACK)).astype(F32)
    flat = lambda part: part.transpose(1, 0, 2).reshape(own_rows, -1)
    pair_sum = lambda part: flat(part.reshape(KV_HEADS, 2, own_rows, HD).sum(axis=1))
    owned = jnp.concatenate(
        [
            flat(got[:, :, :HD]),
            pair_sum(got[:, :, HD : 2 * HD]),
            pair_sum(got[:, :, 2 * HD : HEAD_COLS]),
            out_own.astype(F32),
            got[:, :, HEAD_COLS:].sum(axis=0),
            jnp.zeros((own_rows, HD), F32),
        ],
        axis=1,
    ).astype(BF16)
    width = owned.shape[1]
    share = jnp.sum(
        exchange(owned.reshape(REPS, own_rows // REPS, width), "rep").astype(F32), axis=0
    ).astype(BF16)
    owned = exchange(jnp.broadcast_to(share[None], (REPS, *share.shape)), "rep")
    owned = owned.reshape(own_rows, width).astype(F32)
    base = q_width + 2 * kv_width + D
    four = HD // SHARDS
    return (
        jnp.concatenate(outputs, axis=0),
        jnp.concatenate(input_grads, axis=0),
        owned[:, : base - D],
        owned[:, base - D : base],
        owned[:, base : base + EXPERTS],
        owned[:, base + EXPERTS + 1],
        owned[:, base + EXPERTS],
        owned[:four, base + EXPERTS + 2],
        owned[:four, base + EXPERTS + 3],
        *(g.astype(F32) for g in grad_experts),
    )


def solution(mesh):
    rows = P(("rep", "shard"), None)
    rep, split, vector = P("rep", None, None), P("shard", None), P("shard")
    expert = P("shard", None, None)
    return jax.shard_map(
        local,
        mesh=mesh,
        in_specs=(rows,) * 3 + (rep,) * 2 + (split,) * 3 + (vector,) * 4 + (expert,) * 3,
        out_specs=(rows,) * 2 + (split,) * 3 + (vector,) * 4 + (expert,) * 3,
        check_vma=False,
    )
```

time: 1480 us -> 589 us (0.40)
  waiting for transfers between devices: 553 us -> 154 us
  local copies, waits for them, and re-layouts: 338 us -> 50.8 us
  matrix products: 221 us -> 28.5 us
  Pallas kernels: 0 us -> 133 us
  blocking collectives: 154 us -> 58 us
  other arithmetic: 139 us -> 53.7 us
  starting transfers between devices: 45.4 us -> 86.7 us
    psum x1, waiting for transfers between devices: 205 us -> 0.62 us  [local(): grad_experts = lax.psum(tuple(grads), 'rep')]
    dot_general x48 -> x18, matrix products: 221 us -> 28.5 us  [the longest x16 28.1 us: mm(): lax.dot_general(a, b, (((left,), (right,)), ((), ())), preferred_element_...]
    reduce_scatter x4 -> x0, waiting for transfers between devices: 139 us -> none  [the longest x1 75.3 us: local(): lax.psum_scatter(front_totals[0], 'shard', scatter_dimension=0, tiled=True)]
    pallas_call x0 -> x18, Pallas kernels: none -> 133 us  [the longest x2 58.2 us: experts_step(): pl.pallas_call(functools.partial(expert_kernel, later=later, kinds=kinds,...]
    reshape x18 -> x5, local copies, waits for them, and re-layouts: 102 us -> 2.72 us  [the longest x1 2.07 us: local(): hits_all = hits_all.reshape(SHARDS, 2 * MICRO, EXPERTS, TPD)[ordered]]
    gather x4 -> x5, local copies, waits for them, and re-layouts: 84.9 us -> 5.56 us  [the longest x1 2.45 us: local(): hits_all = hits_all.reshape(SHARDS, 2 * MICRO, EXPERTS, TPD)[ordered]]
    all_to_all x8 -> x12, waiting for transfers between devices: 105 us -> 40.8 us  [exchange(): lax.all_to_all(values, axis, split_axis=0, concat_axis=0, tiled=True, axi...]
    unnamed x2 -> x0, blocking collectives: 62 us -> none
  transfers between devices with their start and end apart: 20 -> 35, of which waited for: 13 -> 17; matrix products, arithmetic and copies ran while one was open for 33% -> 20% of each run, Pallas kernels for 0% -> 23%
where the time goes in v1:
time: 589 us; the launch traced here: 580 us
  waiting for transfers between devices  154 us (26%)
  Pallas kernels  133 us (23%)
  starting transfers between devices  86.7 us (15%)
  blocking collectives  58 us (10%)
  other arithmetic  53.7 us (9%)
  local copies, waits for them, and re-layouts  50.8 us (9%)
  matrix products  28.5 us (5%)
  between operations  15.4 us (3%)
    all_to_all x12, starting transfers between devices, exchange(): lax.all_to_all(values, axis, split_axis=0, concat_axis=0, tiled=True, axi...  63.3 us
    all_gather x3, waiting for transfers between devices, gather(): return lax.all_gather(values, 'shard', axis=0)  59.1 us
    pallas_call x2, Pallas kernels, experts_step(): pl.pallas_call(functools.partial(expert_kernel, later=later, kinds=kinds,...  58.2 us
    all_to_all x2, blocking collectives, exchange(): lax.all_to_all(values, axis, split_axis=0, concat_axis=0, tiled=True, axi...  58 us
    ppermute x18, waiting for transfers between devices, permute(): return lax.ppermute(values, 'shard', pairs)  53 us
    pallas_call x2, Pallas kernels, attn_bwd(): pl.pallas_call(attn_bwd_kernel, grid=(1,), in_specs=[whole(*grad.shape)]...  43.3 us
    all_to_all x12, waiting for transfers between devices, exchange(): lax.all_to_all(values, axis, split_axis=0, concat_axis=0, tiled=True, axi...  40.8 us
    pallas_call x1, Pallas kernels, attn_fwd(): pl.pallas_call(attn_fwd_kernel, grid=(MICRO, CHUNKS), in_specs=[pl.BlockS...  31.3 us
  transfers between devices with their start and end apart: 35, of which 17 were waited for; matrix products, arithmetic and copies ran while one was open for 20% of the time, Pallas kernels for 23%

profile of v1, /device:TPU:1, one launch (start us, length us, event | category | flops | bytes accessed | tf_op | source)
XLA Modules:
  0.0 580.2 jit_solution(8310651816743534788)
XLA Ops:
  10.7 6.8 %all-to-all-start = ((bf16[16,64,256]{2,1,0:T(8,128)(2,1)}), bf16[16,64,256]{2,1,0:T(8,128)(2,1)S(1)}, u32[]{:S(2)}, u32[]{:S(2)}) async-start(bf16[16,64,256]{2,1,0:T(8,128)(2,1)} %copy.333), calls=%async_computation | async-start | bytes 1048576 | tf_op jit(solution)/shard_map/all_to_all | solution.py:439
  22.2 6.0 %all-to-all-done = bf16[16,64,256]{2,1,0:T(8,128)(2,1)S(1)} async-done(((bf16[16,64,256]{2,1,0:T(8,128)(2,1)}), bf16[16,64,256]{2,1,0:T(8,128)(2,1)S(1)}, u32[]{:S(2)}, u32[]{:S(2)}) %all-to-all-start) | async-done | bytes 524320 | tf_op jit(solution)/shard_map/all_to_all | solution.py:439
  28.2 39.9 %all-gather.10.cloned.1.call-done = bf16[4096,1024]{1,0:T(8,128)(2,1)} async-done(((bf16[256,1024]{1,0:T(8,128)(2,1)}), bf16[4096,1024]{1,0:T(8,128)(2,1)}) %all-gather.10.cloned.1.call-update) | async-done | bytes 8388624 | tf_op jit(solution)/shard_map/all_gather | solution.py:400
  72.2 31.3 %attn_fwd.1 = (bf16[2,2048,1024]{2,1,0:T(8,128)(2,1)}, f32[2,8,128,256]{3,2,1,0:T(8,128)}, bf16[2,2048,128]{2,1,0:T(8,128)(2,1)}, bf16[2,8,64,256]{3,2,1,0:T(8,1...) custom-call(bf16[16,256,1024]{2,1,0:T(8,128)(2,1)} %after.14.x_ref.e, ...), custom_call_target="tpu_custom_call" | custom-call | flops 1000000 | bytes 1000000 | tf_op jit(solution)/shard_map/attn_fwd/pallas_call | solution.py:141
  103.5 18.7 %all_to_all.70.values_ref = bf16[16,64,256]{2,1,0:T(8,128)(2,1)} all-to-all(bf16[16,64,256]{2,1,0:T(8,128)(2,1)} %get-tuple-element.43), channel_id=1, replica_groups=mesh['rep'=8,'shard'=16] {'shard'}, dimensions={0} | all-to-all | bytes 1048576 | tf_op jit(solution)/shard_map/all_to_all | solution.py:439
  122.2 19.1 %all-gather.12.cloned.1.call-done = bf16[5376,1024]{1,0:T(8,128)(2,1)} async-done(((bf16[336,1024]{1,0:T(8,128)(2,1)}), bf16[5376,1024]{1,0:T(8,128)(2,1)}) %all-gather.12.cloned.1.call-update) | async-done | bytes 11010064 | tf_op jit(solution)/shard_map/all_gather | solution.py:400
  148.2 39.3 %all_to_all.71.refs_0_ = bf16[8,128,1024]{2,1,0:T(8,128)(2,1)S(1)} all-to-all(bf16[8,128,1024]{2,1,0:T(8,128)(2,1)S(1)} %broadcast_in_dim.119), channel_id=1, replica_groups={{0,2,4,6,8,10,12,14},{1,3,5,7,9,11,13,15},{16,18,20,22,24,26,28,30},{17..., dimensions={0} | all-to-all | bytes 4194304 | tf_op jit(solution)/shard_map/all_to_all | solution.py:439
  187.5 4.4 collective-permute-start
  205.1 28.5 %experts.2 = (bf16[8,128,1024]{2,1,0:T(8,128)(2,1)}, bf16[8,128,1024]{2,1,0:T(8,128)(2,1)}, bf16[8,128,1024]{2,1,0:T(8,128)(2,1)}, bf16[8,128,1024]{2,1,0:T(8,12...) custom-call(s32[1]{0:T(128)} %bitcast.20.core_ref, ...), custom_call_target="tpu_custom_call" | custom-call | flops 1000000 | bytes 1000000 | tf_op jit(solution)/shard_map/experts/pallas_call | solution.py:365
  236.1 4.3 all-to-all-start.4
  246.2 4.5 all-to-all-start.3
  257.4 29.7 %experts.3 = (bf16[8,128,1024]{2,1,0:T(8,128)(2,1)}, bf16[8,128,1024]{2,1,0:T(8,128)(2,1)}, bf16[8,128,1024]{2,1,0:T(8,128)(2,1)}, bf16[8,128,1024]{2,1,0:T(8,12...) custom-call(s32[1]{0:T(128)} %bitcast.20.core_ref, ...), custom_call_target="tpu_custom_call" | custom-call | flops 1000000 | bytes 1000000 | tf_op jit(solution)/shard_map/experts/pallas_call | solution.py:365
  294.5 5.8 all-to-all-start.5
  301.5 6.0 %all-to-all-done.5.earlier_ref.values_ref = bf16[16,64,128]{2,1,0:T(8,128)(2,1)S(1)} async-done(((bf16[16,64,128]{2,1,0:T(8,128)(2,1)}), bf16[16,64,128]{2,1,0:T(8,128)(2,1)S(1)}, u32[]{:S(2)}, u32[]{:S(2)}) %all-to-all-start.5) | async-done | bytes 262176 | tf_op jit(solution)/shard_map/all_to_all | solution.py:439
  307.5 4.4 all-to-all-start.7
  311.9 4.6 add_convert_fusion.3.earlier_ref
  325.2 21.6 %attn_bwd.2 = (bf16[16,192,128]{2,1,0:T(8,128)(2,1)}, f32[192,1024]{1,0:T(8,128)}, f32[128,128]{1,0:T(8,128)}) custom-call(bf16[16,64,128]{2,1,0:T(8,128)(2,1)} %after.18.grad_ref, f32[2,8,64,256]{3,2,1,0:T(8,128)} %get-tuple-element.54.outf_ref, f32[2,8,1,256]{3,2,1,0:T(1,128)} %get-tuple-element.55.inv_ref, ...), custom_call_target="tpu_custom_call" | custom-call | flops 1000000 | bytes 1000000 | tf_op jit(solution)/shard_map/attn_bwd/pallas_call | solution.py:246
  355.2 8.1 %all-to-all-start.8 = ((bf16[16,64,128]{2,1,0:T(8,128)(2,1)}), bf16[16,64,128]{2,1,0:T(8,128)(2,1)S(1)}, u32[]{:S(2)}, u32[]{:S(2)}) async-start(bf16[16,64,128]{2,1,0:T(8,128)(2,1)} %bitcast.48), calls=%async_computation.8 | async-start | bytes 524288 | tf_op jit(solution)/shard_map/all_to_all | solution.py:439
  363.6 6.9 %all-to-all-done.8.earlier_ref.grad_ref = bf16[16,64,128]{2,1,0:T(8,128)(2,1)S(1)} async-done(((bf16[16,64,128]{2,1,0:T(8,128)(2,1)}), bf16[16,64,128]{2,1,0:T(8,128)(2,1)S(1)}, u32[]{:S(2)}, u32[]{:S(2)}) %all-to-all-start.8) | async-done | bytes 262176 | tf_op jit(solution)/shard_map/all_to_all | solution.py:439
  371.2 4.8 all-to-all-start.9
  380.5 21.6 %attn_bwd.3 = (bf16[16,192,128]{2,1,0:T(8,128)(2,1)}, f32[192,1024]{1,0:T(8,128)}, f32[128,128]{1,0:T(8,128)}) custom-call(bf16[16,64,128]{2,1,0:T(8,128)(2,1)} %copy-done.14, f32[2,8,64,256]{3,2,1,0:T(8,128)} %get-tuple-element.54.outf_ref, f32[2,8,1,256]{3,2,1,0:T(1,128)} %get-tuple-element.55.inv_ref, bf16[2,2048,128]{2,1,0:T(8,128)(2,1)} %get-tuple-element.56.key_ref, ...), custom_call_target="tpu_custom_call" | custom-call | flops 1000000 | bytes 1000000 | tf_op jit(solution)/shard_map/attn_bwd/pallas_call | solution.py:246
  402.1 5.7 all-to-all-start.10
  447.7 8.0 %collective-permute-done.10 = bf16[2,128,1024]{2,1,0:T(8,128)(2,1)S(1)} collective-permute-done((bf16[2,128,1024]{2,1,0:T(8,128)(2,1)S(1)}, bf16[2,128,1024]{2,1,0:T(8,128)(2,1)S(1)}, u32[]{:S(2)}, u32[]{:S(2)}) %collective-permute-start.10) | collective-permute-done | bytes 524320 | tf_op jit(solution)/shard_map/ppermute | solution.py:428
  458.3 8.5 %collective-permute-done.11 = bf16[2,128,1024]{2,1,0:T(8,128)(2,1)S(1)} collective-permute-done((bf16[2,128,1024]{2,1,0:T(8,128)(2,1)S(1)}, bf16[2,128,1024]{2,1,0:T(8,128)(2,1)S(1)}, u32[]{:S(2)}, u32[]{:S(2)}) %collective-permute-start.11) | collective-permute-done | bytes 524320 | tf_op jit(solution)/shard_map/ppermute | solution.py:428
  471.4 7.2 %collective-permute-done.4 = bf16[2,128,1024]{2,1,0:T(8,128)(2,1)S(1)} collective-permute-done((bf16[2,128,1024]{2,1,0:T(8,128)(2,1)S(1)}, bf16[2,128,1024]{2,1,0:T(8,128)(2,1)S(1)}, u32[]{:S(2)}, u32[]{:S(2)}) %collective-permute-start.4) | collective-permute-done | bytes 524320 | tf_op jit(solution)/shard_map/ppermute | solution.py:428
  478.6 10.9 %collective-permute-done.5 = bf16[2,128,1024]{2,1,0:T(8,128)(2,1)S(1)} collective-permute-done((bf16[2,128,1024]{2,1,0:T(8,128)(2,1)S(1)}, bf16[2,128,1024]{2,1,0:T(8,128)(2,1)S(1)}, u32[]{:S(2)}, u32[]{:S(2)}) %collective-permute-start.5) | collective-permute-done | bytes 524320 | tf_op jit(solution)/shard_map/ppermute | solution.py:428
  497.5 6.1 %collective-permute-done.7 = bf16[128,1024]{1,0:T(8,128)(2,1)S(1)} collective-permute-done((bf16[128,1024]{1,0:T(8,128)(2,1)S(1)}, bf16[128,1024]{1,0:T(8,128)(2,1)S(1)}, u32[]{:S(2)}, u32[]{:S(2)}) %collective-permute-start.7) | collective-permute-done | bytes 262176 | tf_op jit(solution)/shard_map/ppermute | solution.py:428
  504.7 5.5 all-to-all-start.11
  513.3 12.3 %collective-permute-done.17 = bf16[64,1024]{1,0:T(8,128)(2,1)S(1)} collective-permute-done((bf16[64,1024]{1,0:T(8,128)(2,1)S(1)}, bf16[64,1024]{1,0:T(8,128)(2,1)S(1)}, u32[]{:S(2)}, u32[]{:S(2)}) %collective-permute-start.17) | collective-permute-done | bytes 131104 | tf_op jit(solution)/shard_map/ppermute | solution.py:428
  530.6 5.9 %all-to-all-start.12 = ((bf16[8,8,3200]{2,1,0:T(8,128)(2,1)}), bf16[8,8,3200]{2,1,0:T(8,128)(2,1)S(1)}, u32[]{:S(2)}, u32[]{:S(2)}) async-start(bf16[8,8,3200]{2,1,0:T(8,128)(2,1)} %concatenate.67), calls=%async_computation.12 | async-start | bytes 819200 | tf_op jit(solution)/shard_map/all_to_all | solution.py:439
  537.2 15.2 %all-to-all-done.12 = bf16[8,8,3200]{2,1,0:T(8,128)(2,1)S(1)} async-done(((bf16[8,8,3200]{2,1,0:T(8,128)(2,1)}), bf16[8,8,3200]{2,1,0:T(8,128)(2,1)S(1)}, u32[]{:S(2)}, u32[]{:S(2)}) %all-to-all-start.12) | async-done | bytes 409632 | tf_op jit(solution)/shard_map/all_to_all | solution.py:439
  559.5 4.3 convert_element_type.316
  (335 shorter events, 159.0 us)
Async XLA Ops:
  7.2 60.9 %all-gather.10.cloned.1.call-start = ((), (), s32[]{:S(2)}) async-start(), calls=%async_computation.15 | async-start | bytes 8912896 | tf_op jit(solution)/shard_map/all_gather | solution.py:400
  10.7 17.4 %all-to-all-start = ((bf16[16,64,256]{2,1,0:T(8,128)(2,1)}), bf16[16,64,256]{2,1,0:T(8,128)(2,1)S(1)}, u32[]{:S(2)}, u32[]{:S(2)}) async-start(bf16[16,64,256]{2,1,0:T(8,128)(2,1)} %copy.333), calls=%async_computation | async-start | bytes 1048576 | tf_op jit(solution)/shard_map/all_to_all | solution.py:439
  17.6 123.7 %all-gather.12.cloned.1.call-start = ((), (), s32[]{:S(2)}) async-start(), calls=%async_computation.16 | async-start | bytes 11698176 | tf_op jit(solution)/shard_map/all_gather | solution.py:400
  68.1 182.8 %all-gather.14.cloned.1.call-start = ((), (), s32[]{:S(2)}) async-start(), calls=%async_computation.17 | async-start | bytes 4456448 | tf_op jit(solution)/shard_map/all_gather | solution.py:400
  187.5 13.8 %collective-permute-start = (bf16[8,128,1024]{2,1,0:T(8,128)(2,1)S(1)}, bf16[8,128,1024]{2,1,0:T(8,128)(2,1)}, u32[]{:S(2)}, u32[]{:S(2)}) collective-permute-start(bf16[8,128,1024]{2,1,0:T(8,128)(2,1)S(1)} %all_to_all.71.refs_0_), channel_id=1, source_target_pairs={{0,1},{1,0},{2,3},{3,2},{4,5},{5,4},{6,7},{7,6},{8,9},{9,8},{10,11... | collective-permute-start | bytes 6291464 | tf_op jit(solution)/shard_map/ppermute | solution.py:428
  240.4 189.9 %all-gather.8.cloned.1.call-start = ((), (), s32[]{:S(2)}) async-start(), calls=%async_computation.14 | async-start | bytes 4456448 | tf_op jit(solution)/shard_map/all_gather | solution.py:585
  246.2 43.4 %all-to-all-start.3 = ((bf16[8,128,1024]{2,1,0:T(8,128)(2,1)}), bf16[8,128,1024]{2,1,0:T(8,128)(2,1)}, u32[]{:S(2)}, u32[]{:S(2)}) async-start(bf16[8,128,1024]{2,1,0:T(8,128)(2,1)} %add_convert_fusion.4.refs_0_), calls=%async_computation.3 | async-start | bytes 4194304 | tf_op jit(solution)/shard_map/all_to_all | solution.py:439
  287.2 24.7 %collective-permute-start.2 = (bf16[8,128,1024]{2,1,0:T(8,128)(2,1)}, bf16[8,128,1024]{2,1,0:T(8,128)(2,1)}, u32[]{:S(2)}, u32[]{:S(2)}) collective-permute-start(bf16[8,128,1024]{2,1,0:T(8,128)(2,1)} %get-tuple-element.53), channel_id=1, source_target_pairs={{0,1},{1,0},{2,3},{3,2},{4,5},{5,4},{6,7},{7,6},{8,9},{9,8},{10,11... | collective-permute-start | bytes 6291464 | tf_op jit(solution)/shard_map/ppermute | solution.py:428
  294.5 12.9 %all-to-all-start.5 = ((bf16[16,64,128]{2,1,0:T(8,128)(2,1)}), bf16[16,64,128]{2,1,0:T(8,128)(2,1)S(1)}, u32[]{:S(2)}, u32[]{:S(2)}) async-start(bf16[16,64,128]{2,1,0:T(8,128)(2,1)} %bitcast.300), calls=%async_computation.5 | async-start | bytes 524288 | tf_op jit(solution)/shard_map/all_to_all | solution.py:439
  317.6 31.1 %all-to-all-start.6 = ((bf16[8,128,1024]{2,1,0:T(8,128)(2,1)}), bf16[8,128,1024]{2,1,0:T(8,128)(2,1)S(1)}, u32[]{:S(2)}, u32[]{:S(2)}) async-start(bf16[8,128,1024]{2,1,0:T(8,128)(2,1)} %add_convert_fusion.3.earlier_ref), calls=%async_computation.6 | async-start | bytes 4194304 | tf_op jit(solution)/shard_map/all_to_all | solution.py:439
  355.2 15.3 %all-to-all-start.8 = ((bf16[16,64,128]{2,1,0:T(8,128)(2,1)}), bf16[16,64,128]{2,1,0:T(8,128)(2,1)S(1)}, u32[]{:S(2)}, u32[]{:S(2)}) async-start(bf16[16,64,128]{2,1,0:T(8,128)(2,1)} %bitcast.48), calls=%async_computation.8 | async-start | bytes 524288 | tf_op jit(solution)/shard_map/all_to_all | solution.py:439
  371.2 30.9 %all-to-all-start.9 = ((bf16[16,192,128]{2,1,0:T(8,128)(2,1)}), bf16[16,192,128]{2,1,0:T(8,128)(2,1)}, u32[]{:S(2)}, u32[]{:S(2)}) async-start(bf16[16,192,128]{2,1,0:T(8,128)(2,1)} %after.22), calls=%async_computation.9 | async-start | bytes 1572864 | tf_op jit(solution)/shard_map/all_to_all | solution.py:439
  376.0 183.5 %all-reduce.9.cloned.1.call-start = ((), (), s32[]{:S(2)}) async-start(), calls=%async_computation.18 | async-start | bytes 12582912 | tf_op jit(solution)/shard_map/psum | solution.py:586
  380.2 57.4 %collective-permute-start.8 = (bf16[8,128,1024]{2,1,0:T(8,128)(2,1)}, bf16[8,128,1024]{2,1,0:T(8,128)(2,1)}, u32[]{:S(2)}, u32[]{:S(2)}) collective-permute-start(bf16[8,128,1024]{2,1,0:T(8,128)(2,1)} %after.21), channel_id=1, source_target_pairs={{0,1},{1,0},{2,3},{3,2},{4,5},{5,4},{6,7},{7,6},{8,9},{9,8},{10,11... | collective-permute-start | bytes 6291464 | tf_op jit(solution)/shard_map/ppermute | solution.py:428
  402.1 19.5 %all-to-all-start.10 = ((bf16[16,192,128]{2,1,0:T(8,128)(2,1)}), bf16[16,192,128]{2,1,0:T(8,128)(2,1)}, u32[]{:S(2)}, u32[]{:S(2)}) async-start(bf16[16,192,128]{2,1,0:T(8,128)(2,1)} %get-tuple-element.66), calls=%async_computation.10 | async-start | bytes 1572864 | tf_op jit(solution)/shard_map/all_to_all | solution.py:439
  413.1 77.0 %collective-permute-start.13 = (bf16[8,64,1024]{2,1,0:T(8,128)(2,1)}, bf16[8,64,1024]{2,1,0:T(8,128)(2,1)}, u32[]{:S(2)}, u32[]{:S(2)}) collective-permute-start(bf16[8,64,1024]{2,1,0:T(8,128)(2,1)} %dynamic-slice_bitcast_fusion), channel_id=1, source_target_pairs={{0,1},{1,0},{2,3},{3,2},{4,5},{5,4},{6,7},{7,6},{8,9},{9,8},{10,11... | collective-permute-start | bytes 3145736 | tf_op jit(solution)/shard_map/ppermute | solution.py:428
  413.5 31.1 %collective-permute-start.3 = (bf16[8,128,1024]{2,1,0:T(8,128)(2,1)}, bf16[8,128,1024]{2,1,0:T(8,128)(2,1)}, u32[]{:S(2)}, u32[]{:S(2)}) collective-permute-start(bf16[8,128,1024]{2,1,0:T(8,128)(2,1)} %after.20), channel_id=1, source_target_pairs={{0,1},{1,0},{2,3},{3,2},{4,5},{5,4},{6,7},{7,6},{8,9},{9,8},{10,11... | collective-permute-start | bytes 6291464 | tf_op jit(solution)/shard_map/ppermute | solution.py:428
  440.4 15.3 %collective-permute-start.10 = (bf16[2,128,1024]{2,1,0:T(8,128)(2,1)S(1)}, bf16[2,128,1024]{2,1,0:T(8,128)(2,1)S(1)}, u32[]{:S(2)}, u32[]{:S(2)}) collective-permute-start(bf16[2,128,1024]{2,1,0:T(8,128)(2,1)S(1)} %get-tuple-element.216), channel_id=1, source_target_pairs={{0,4},{1,5},{2,6},{3,7},{4,0},{5,1},{6,2},{7,3},{8,12},{9,13},{10,... | collective-permute-start | bytes 1572872 | tf_op jit(solution)/shard_map/ppermute | solution.py:428
  443.1 23.7 %collective-permute-start.11 = (bf16[2,128,1024]{2,1,0:T(8,128)(2,1)S(1)}, bf16[2,128,1024]{2,1,0:T(8,128)(2,1)S(1)}, u32[]{:S(2)}, u32[]{:S(2)}) collective-permute-start(bf16[2,128,1024]{2,1,0:T(8,128)(2,1)S(1)} %get-tuple-element.215), channel_id=1, source_target_pairs={{0,6},{1,7},{2,0},{3,1},{4,2},{5,3},{6,4},{7,5},{8,14},{9,15},{10,... | collective-permute-start | bytes 1572872 | tf_op jit(solution)/shard_map/ppermute | solution.py:428
  444.0 26.9 %collective-permute-start.9 = (bf16[2,128,1024]{2,1,0:T(8,128)(2,1)S(1)}, bf16[2,128,1024]{2,1,0:T(8,128)(2,1)S(1)}, u32[]{:S(2)}, u32[]{:S(2)}) collective-permute-start(bf16[2,128,1024]{2,1,0:T(8,128)(2,1)S(1)} %get-tuple-element.214), channel_id=1, source_target_pairs={{0,2},{1,3},{2,4},{3,5},{4,6},{5,7},{6,0},{7,1},{8,10},{9,11},{10,... | collective-permute-start | bytes 1572872 | tf_op jit(solution)/shard_map/ppermute | solution.py:428
  447.3 31.3 %collective-permute-start.4 = (bf16[2,128,1024]{2,1,0:T(8,128)(2,1)S(1)}, bf16[2,128,1024]{2,1,0:T(8,128)(2,1)S(1)}, u32[]{:S(2)}, u32[]{:S(2)}) collective-permute-start(bf16[2,128,1024]{2,1,0:T(8,128)(2,1)S(1)} %get-tuple-element.211), channel_id=1, source_target_pairs={{0,2},{1,3},{2,4},{3,5},{4,6},{5,7},{6,0},{7,1},{8,10},{9,11},{10,... | collective-permute-start | bytes 1572872 | tf_op jit(solution)/shard_map/ppermute | solution.py:428
  455.7 33.7 %collective-permute-start.5 = (bf16[2,128,1024]{2,1,0:T(8,128)(2,1)S(1)}, bf16[2,128,1024]{2,1,0:T(8,128)(2,1)S(1)}, u32[]{:S(2)}, u32[]{:S(2)}) collective-permute-start(bf16[2,128,1024]{2,1,0:T(8,128)(2,1)S(1)} %get-tuple-element.213), channel_id=1, source_target_pairs={{0,4},{1,5},{2,6},{3,7},{4,0},{5,1},{6,2},{7,3},{8,12},{9,13},{10,... | collective-permute-start | bytes 1572872 | tf_op jit(solution)/shard_map/ppermute | solution.py:428
  466.8 22.6 %collective-permute-start.6 = (bf16[2,128,1024]{2,1,0:T(8,128)(2,1)S(1)}, bf16[2,128,1024]{2,1,0:T(8,128)(2,1)S(1)}, u32[]{:S(2)}, u32[]{:S(2)}) collective-permute-start(bf16[2,128,1024]{2,1,0:T(8,128)(2,1)S(1)} %get-tuple-element.212), channel_id=1, source_target_pairs={{0,6},{1,7},{2,0},{3,1},{4,2},{5,3},{6,4},{7,5},{8,14},{9,15},{10,... | collective-permute-start | bytes 1572872 | tf_op jit(solution)/shard_map/ppermute | solution.py:428
  471.3 26.2 %collective-permute-start.12 = (bf16[128,1024]{1,0:T(8,128)(2,1)S(1)}, bf16[128,1024]{1,0:T(8,128)(2,1)S(1)}, u32[]{:S(2)}, u32[]{:S(2)}) collective-permute-start(bf16[128,1024]{1,0:T(8,128)(2,1)S(1)} %fusion.30), channel_id=1, source_target_pairs={{0,8},{1,9},{2,10},{3,11},{4,12},{5,13},{6,14},{7,15},{8,0},{9,1},... | collective-permute-start | bytes 786440 | tf_op jit(solution)/shard_map/ppermute | solution.py:428
  489.9 13.7 %collective-permute-start.7 = (bf16[128,1024]{1,0:T(8,128)(2,1)S(1)}, bf16[128,1024]{1,0:T(8,128)(2,1)S(1)}, u32[]{:S(2)}, u32[]{:S(2)}) collective-permute-start(bf16[128,1024]{1,0:T(8,128)(2,1)S(1)} %fusion.29), channel_id=1, source_target_pairs={{0,8},{1,9},{2,10},{3,11},{4,12},{5,13},{6,14},{7,15},{8,0},{9,1},... | collective-permute-start | bytes 786440 | tf_op jit(solution)/shard_map/ppermute | solution.py:428
  492.9 17.4 %collective-permute-start.14 = (bf16[2,64,1024]{2,1,0:T(8,128)(2,1)}, bf16[2,64,1024]{2,1,0:T(8,128)(2,1)}, u32[]{:S(2)}, u32[]{:S(2)}) collective-permute-start(bf16[2,64,1024]{2,1,0:T(8,128)(2,1)} %get-tuple-element.219), channel_id=1, source_target_pairs={{0,2},{1,3},{2,4},{3,5},{4,6},{5,7},{6,0},{7,1},{8,10},{9,11},{10,... | collective-permute-start | bytes 786440 | tf_op jit(solution)/shard_map/ppermute | solution.py:428
  494.1 16.1 %collective-permute-start.15 = (bf16[2,64,1024]{2,1,0:T(8,128)(2,1)}, bf16[2,64,1024]{2,1,0:T(8,128)(2,1)}, u32[]{:S(2)}, u32[]{:S(2)}) collective-permute-start(bf16[2,64,1024]{2,1,0:T(8,128)(2,1)} %get-tuple-element.221), channel_id=1, source_target_pairs={{0,4},{1,5},{2,6},{3,7},{4,0},{5,1},{6,2},{7,3},{8,12},{9,13},{10,... | collective-permute-start | bytes 786440 | tf_op jit(solution)/shard_map/ppermute | solution.py:428
  496.5 13.7 %collective-permute-start.16 = (bf16[2,64,1024]{2,1,0:T(8,128)(2,1)S(1)}, bf16[2,64,1024]{2,1,0:T(8,128)(2,1)}, u32[]{:S(2)}, u32[]{:S(2)}) collective-permute-start(bf16[2,64,1024]{2,1,0:T(8,128)(2,1)S(1)} %get-tuple-element.220), channel_id=1, source_target_pairs={{0,6},{1,7},{2,0},{3,1},{4,2},{5,3},{6,4},{7,5},{8,14},{9,15},{10,... | collective-permute-start | bytes 786440 | tf_op jit(solution)/shard_map/ppermute | solution.py:428
  504.7 20.9 %all-to-all-start.11 = ((bf16[16,64,256]{2,1,0:T(8,128)(2,1)}), bf16[16,64,256]{2,1,0:T(8,128)(2,1)S(1)}, u32[]{:S(2)}, u32[]{:S(2)}) async-start(bf16[16,64,256]{2,1,0:T(8,128)(2,1)} %bitcast.286), calls=%async_computation.11 | async-start | bytes 1048576 | tf_op jit(solution)/shard_map/all_to_all | solution.py:439
  511.6 13.9 %collective-permute-start.17 = (bf16[64,1024]{1,0:T(8,128)(2,1)S(1)}, bf16[64,1024]{1,0:T(8,128)(2,1)S(1)}, u32[]{:S(2)}, u32[]{:S(2)}) collective-permute-start(bf16[64,1024]{1,0:T(8,128)(2,1)S(1)} %fusion.46), channel_id=1, source_target_pairs={{0,8},{1,9},{2,10},{3,11},{4,12},{5,13},{6,14},{7,15},{8,0},{9,1},... | collective-permute-start | bytes 393224 | tf_op jit(solution)/shard_map/ppermute | solution.py:428
  530.6 21.8 %all-to-all-start.12 = ((bf16[8,8,3200]{2,1,0:T(8,128)(2,1)}), bf16[8,8,3200]{2,1,0:T(8,128)(2,1)S(1)}, u32[]{:S(2)}, u32[]{:S(2)}) async-start(bf16[8,8,3200]{2,1,0:T(8,128)(2,1)} %concatenate.67), calls=%async_computation.12 | async-start | bytes 819200 | tf_op jit(solution)/shard_map/all_to_all | solution.py:439
  553.3 16.5 %all-to-all-start.13 = ((bf16[8,8,3200]{2,1,0:T(8,128)(2,1)}), bf16[8,8,3200]{2,1,0:T(8,128)(2,1)S(1)}, u32[]{:S(2)}, u32[]{:S(2)}) async-start(bf16[8,8,3200]{2,1,0:T(8,128)(2,1)} %broadcast_in_dim.132), calls=%async_computation.13 | async-start | bytes 819200 | tf_op jit(solution)/shard_map/all_to_all | solution.py:439
  (54 other events, 392.7 us)
Sparse Core Ops, SparseCore 0:
  9.8 58.2 all-gather.9
  70.4 70.8 all-gather.11
  148.0 53.6 all-gather.13
  242.7 59.1 all-gather.7
  379.3 180.1 all-reduce.8

commit v2 on v1

--- a/solution.py
+++ b/solution.py
@@ -27,6 +27,7 @@
 ROWS = SHARDS * SLOTS
 PART = 4
 PARTS = SHARDS // PART
+TALL = TPD + 16
 CHUNK = 256
 CHUNKS = G // CHUNK
 HEAD_COLS = 3 * HD
@@ -261,18 +262,24 @@
     )(grad, *operands)
 
 
+def routed_softmax(logits, hits):
+    top = jnp.max(jnp.where(hits, logits, -jnp.inf), axis=0, keepdims=True)
+    powers = jnp.where(hits, jnp.exp(jnp.where(hits, logits - top, 0.0)), 0.0)
+    return powers / jnp.sum(powers, axis=0, keepdims=True)
+
+
 def expert_kernel(core_ref, *refs, later, kinds, waits):
     refs = refs[waits:]
     rows_refs, refs = refs[: kinds[0]], refs[kinds[0] :]
     grads_refs, refs = refs[: kinds[1]], refs[kinds[1] :]
-    slot_ref, gate_ref, wg_ref, wu_ref, wd_ref, *refs = refs
+    slot_ref, hit_ref, router_ref, wg_ref, wu_ref, wd_ref, *refs = refs
     before_refs = (None,) * 3
     if later:
         before_refs = (refs[2], refs[0], refs[1])
         refs = refs[3:]
     out_refs, back_refs = refs[:2], refs[2:4]
-    route_ref, gg_ref, gu_ref, gd_ref = refs[4:8]
-    xs, cs, ps, ys, ds = refs[8:]
+    gg_ref, gu_ref, gd_ref = refs[4:7]
+    xs, cs, ps, ys, ds = refs[7:]
     step = pl.program_id(0)
     slots = lax.broadcasted_iota(jnp.int32, (SLOTS, TPD), 0).astype(F32)
 
@@ -291,10 +298,14 @@
             hots = [hot_of(e, source) for e in range(LOCAL_EXPERTS)]
             low = jnp.concatenate(hots, axis=0).astype(BF16)
             shape = (LOCAL_EXPERTS, SLOTS, D)
-            xs[:, source] = mm(low, block(rows_refs, k), 1, 0).astype(BF16).reshape(shape)
+            rows = block(rows_refs, k)
+            xs[:, source] = mm(low, rows, 1, 0).astype(BF16).reshape(shape)
             cs[:, source] = mm(low, block(grads_refs, k), 1, 0).astype(BF16).reshape(shape)
+            gates = routed_softmax(mm(router_ref[...], rows, 1, 1), hit_ref[source] > 0)
+            named = lax.broadcasted_iota(jnp.int32, (EXPERTS, TPD), 0) - core_ref[1]
             for e in range(LOCAL_EXPERTS):
-                gate = jnp.where(hots[e], gate_ref[e, pl.ds(source, 1), :], 0.0)
+                gate = jnp.sum(jnp.where(named == e, gates, 0.0), axis=0, keepdims=True)
+                gate = jnp.where(hots[e], gate, 0.0)
                 ps[e, source] = jnp.broadcast_to(
                     jnp.sum(gate, axis=1, keepdims=True), (SLOTS, TPD)
                 )
@@ -336,28 +347,36 @@
             source = (step - PARTS - LOCAL_EXPERTS) * PART + k
             hots = [hot_of(e, source) for e in range(LOCAL_EXPERTS)]
             low = jnp.concatenate(hots, axis=0).astype(BF16)
-            back_refs[k % 2][k // 2] = mm(low, ds[source].reshape(-1, D), 0, 0).astype(BF16)
+            back_refs[k % 2][k // 2, :TPD] = mm(low, ds[source].reshape(-1, D), 0, 0).astype(BF16)
             out_refs[k % 2][k // 2] = mm(low, ys[source].reshape(-1, D), 0, 0).astype(BF16)
+            pieces = []
             for e in range(LOCAL_EXPERTS):
-                route_ref[e, pl.ds(source, 1), :] = jnp.sum(
-                    jnp.where(hots[e], ps[e, source], 0.0), axis=0, keepdims=True
-                )
-
-
-def experts_step(waits, m, core, rows, grads, slot, gate, w_gate, w_up, w_down, previous):
+                route = jnp.where(hots[e], ps[e, source], 0.0)
+                route = jnp.sum(route, axis=0, keepdims=True)
+                high = route.astype(BF16).astype(F32)
+                pieces += [high, route - high]
+            lanes = jnp.concatenate(pieces, axis=1)
+            row = jnp.concatenate(
+                [jnp.where(core_ref[0] == c, lanes, 0.0) for c in range(2)], axis=1
+            )
+            place = lax.broadcasted_iota(jnp.int32, (TALL - TPD, D), 0)
+            back_refs[k % 2][k // 2, TPD:] = jnp.where(place == 0, row, 0.0).astype(BF16)
+
+
+def experts_step(waits, core, rows, grads, slot, hit, router, w_gate, w_up, w_down, previous):
     later = previous is not None
     whole = lambda *shape: pl.BlockSpec(shape, lambda i, at: (0,) * len(shape))
     first = lambda i, at: (jnp.minimum(i, PARTS - 1), 0, 0)
     kinds = (len(rows), 1)
-    of_micro = lambda i, at: (jnp.minimum(i, PARTS - 1), m, 0)
+    second = lambda i, at: (jnp.minimum(i, PARTS - 1), 1 if later else 0, 0)
     last = lambda i, at: (jnp.maximum(i - PARTS - LOCAL_EXPERTS, 0), 0, 0)
     each = lambda *shape: pl.BlockSpec(
         (1, *shape), lambda i, at: (jnp.clip(i - PARTS, 0, LOCAL_EXPERTS - 1), 0, 0)
     )
     weight_specs = [each(D, FF), each(D, FF), each(FF, D)]
     shapes = [
-        *[((CHIPS, TPD, D), BF16)] * 4,
-        ((LOCAL_EXPERTS, SHARDS, TPD), F32),
+        *[((CHIPS, TPD, D), BF16)] * 2,
+        *[((CHIPS, TALL, D), BF16)] * 2,
         (w_gate.shape, BF16),
         (w_up.shape, BF16),
         (w_down.shape, BF16),
@@ -370,15 +389,16 @@
             in_specs=[
                 *[pl.BlockSpec(memory_space=pl.ANY)] * len(waits),
                 *[pl.BlockSpec((PART // len(rows), TPD, D), first)] * len(rows),
-                pl.BlockSpec((PART, TPD, D), of_micro),
+                pl.BlockSpec((PART, TPD, D), second),
             whole(LOCAL_EXPERTS, SHARDS, TPD),
-            whole(LOCAL_EXPERTS, SHARDS, TPD),
+            whole(SHARDS, EXPERTS, TPD),
+            whole(EXPERTS, D),
         ]
         + weight_specs
         + (weight_specs if later else []),
         out_specs=[
-            *[pl.BlockSpec((PART // 2, TPD, D), last)] * 4,
-            whole(LOCAL_EXPERTS, SHARDS, TPD),
+            *[pl.BlockSpec((PART // 2, TPD, D), last)] * 2,
+            *[pl.BlockSpec((PART // 2, TALL, D), last)] * 2,
         ]
         + weight_specs,
         scratch_shapes=[
@@ -393,7 +413,7 @@
         compiler_params=pltpu.CompilerParams(vmem_limit_bytes=60 * MIB),
         cost_estimate=BRIEF,
         name="experts",
-    )(core, *waits, *rows, grads, slot, gate, w_gate, w_up, w_down, *(previous if later else ()))
+    )(core, *waits, *rows, grads, slot, hit, router, w_gate, w_up, w_down, *(previous if later else ()))
 
 
 def gather(values):
@@ -428,38 +448,261 @@
     return lax.ppermute(values, "shard", pairs)
 
 
-def gather_cores(values):
-    like = exchange(
-        jnp.broadcast_to(values[None], (CHIPS, *values.shape)), groups=SAME_CORE
-    )
-    return like, permute(like, OTHER_CORE)
-
-
 def exchange(values, axis="shard", groups=None):
     return lax.all_to_all(
         values, axis, split_axis=0, concat_axis=0, tiled=True, axis_index_groups=groups
     )
 
 
+def call(kernel, name, shapes, *operands, scalars=(), waits=(), specs=None):
+    count, held = len(operands), len(scalars)
+    specs = dict(specs or {})
+    whole = lambda shape: pl.BlockSpec(shape, lambda i, *_: (0,) * len(shape))
+
+    def body(*refs):
+        kernel(*refs[: held + count], *refs[held + count + len(waits) :])
+
+    return pl.pallas_call(
+        body,
+        grid_spec=pltpu.PrefetchScalarGridSpec(
+            num_scalar_prefetch=held,
+            grid=(1,),
+            in_specs=[specs.get(i, whole(v.shape)) for i, v in enumerate(operands)]
+            + [pl.BlockSpec(memory_space=pl.ANY)] * len(waits),
+            out_specs=[whole(shape) for shape, _ in shapes],
+        ),
+        out_shape=[jax.ShapeDtypeStruct(shape, dtype) for shape, dtype in shapes],
+        compiler_params=pltpu.CompilerParams(vmem_limit_bytes=60 * MIB),
+        cost_estimate=BRIEF,
+        name=name,
+    )(*scalars, *operands, *waits)
+
+
+def block(shape, *index):
+    return pl.BlockSpec(shape, lambda i, *_: index)
+
+
+OUT_ROWS = block((SHARDS, D // SHARDS, D), 0, 2, 0)
+
+
+def mid_kernel(att_ref, wout_ref, x_ref, gain_ref, cot_ref, wqkv_ref, mid_ref, first_ref, second_ref):
+    mid = x_ref[...].astype(F32) + mm(att_ref[...], wout_ref[...].reshape(HEADS * HD, D), 0, 0)
+    mid_ref[...] = mid
+    moe_in = (mid * rms_scale(mid) * gain_ref[...]).astype(BF16)
+    first_ref[...] = jnp.broadcast_to(moe_in[None, :TPD], (CHIPS, TPD, D))
+    own = D // SHARDS
+    second_ref[:TPD] = moe_in[TPD:]
+    second_ref[TPD : 2 * TPD] = cot_ref[TPD:]
+    second_ref[2 * TPD : 2 * TPD + own] = wqkv_ref[:, :D]
+    second_ref[2 * TPD + own :] = wqkv_ref[:, D:]
+
+
+def add_kernel(x_ref, *refs, pairs):
+    step = pl.program_id(0)
+    del x_ref
+    total = [
+        (refs[2 * i][...].astype(F32) + refs[2 * i + 1][...].astype(F32)).astype(BF16)
+        for i in range(pairs)
+    ]
+    out_refs = refs[2 * pairs :]
+    if len(out_refs) == 1:
+        out_refs[0][...] = total[0]
+        return
+    for k, out_ref in enumerate(out_refs):
+
+        @pl.when(step == k)
+        def put(out_ref=out_ref):
+            for i in range(pairs):
+                out_ref[i] = total[i][:, 0]
+
+
 def sum_cores(keep, give):
-    return (keep.astype(F32) + permute(give, OTHER_CORE).astype(F32)).astype(BF16)
-
-
-def sum_by_permutes(keep, give, shard):
-    x, y = shard % 8 // 2, shard // 8
-    chip = sum_cores(keep, give).reshape(2, 4, *keep.shape[1:])
-    column = lambda k: lax.dynamic_index_in_dim(chip, (x + k) % 4, 1, keepdims=False)
-    total = column(0).astype(F32)
-    for k, shift in enumerate(X_SHIFTS):
-        total = total + permute(column(k + 1), shift).astype(F32)
-    row = lambda k: lax.dynamic_index_in_dim(total, k, 0, keepdims=False)
-    return row(y) + permute(row(1 - y).astype(BF16), Y_SWAP).astype(F32)
-
-
-def routed_softmax(logits, hits):
-    top = jnp.max(jnp.where(hits, logits, -jnp.inf), axis=0, keepdims=True)
-    powers = jnp.where(hits, jnp.exp(jnp.where(hits, logits - top, 0.0)), 0.0)
-    return powers / jnp.sum(powers, axis=0, keepdims=True)
+    parts = 4
+    spec = pl.BlockSpec((CHIPS // parts, *keep.shape[1:]), lambda i, at: (i, 0, 0))
+    return pl.pallas_call(
+        functools.partial(add_kernel, pairs=1),
+        grid_spec=pltpu.PrefetchScalarGridSpec(
+            num_scalar_prefetch=1, grid=(parts,), in_specs=[spec] * 2, out_specs=[spec]
+        ),
+        out_shape=[jax.ShapeDtypeStruct(keep.shape, BF16)],
+        cost_estimate=BRIEF,
+        name="sum_cores",
+    )(jnp.zeros((1,), jnp.int32), keep, permute(give, OTHER_CORE))[0]
+
+
+def sum_cores_by_x(pairs, shard):
+    own = pairs[0][0].shape[1:]
+    spec = pl.BlockSpec((2, 1, *own), lambda i, at: (0, (at[0] + i) % 4, 0, 0))
+    shape = (len(pairs), 2, *own)
+    whole = pl.BlockSpec(shape, lambda i, at: (0,) * len(shape))
+    operands = []
+    for keep, give in pairs:
+        operands += [keep.reshape(2, 4, *own), permute(give, OTHER_CORE).reshape(2, 4, *own)]
+    return pl.pallas_call(
+        functools.partial(add_kernel, pairs=len(pairs)),
+        grid_spec=pltpu.PrefetchScalarGridSpec(
+            num_scalar_prefetch=1,
+            grid=(4,),
+            in_specs=[spec] * len(operands),
+            out_specs=[whole] * 4,
+        ),
+        out_shape=[jax.ShapeDtypeStruct(shape, BF16)] * 4,
+        compiler_params=pltpu.CompilerParams(vmem_limit_bytes=60 * MIB),
+        cost_estimate=BRIEF,
+        name="sum_cores_by_x",
+    )((shard % 8 // 2).reshape(1), *operands)
+
+
+def along_x_kernel(y_ref, a_ref, b_ref, c_ref, d_ref, keep_ref, give_ref):
+    total = sum(ref[...].astype(F32) for ref in (a_ref, b_ref, c_ref, d_ref))
+    own = y_ref[0] == 0
+    keep_ref[...] = jnp.where(own, total[:, 0], total[:, 1])
+    give_ref[...] = jnp.where(own, total[:, 1], total[:, 0]).astype(BF16)
+
+
+def send_along_x(columns, wait):
+    came = [permute(after(c, wait), shift) for c, shift in zip(columns[1:], X_SHIFTS)]
+    return [columns[0], *came]
+
+
+def sum_along_x(came, shard, wait):
+    shape = (came[0].shape[0], *came[0].shape[2:])
+    return call(
+        along_x_kernel,
+        "sum_along_x",
+        [(shape, F32), (shape, BF16)],
+        *came,
+        scalars=[(shard // 8).reshape(1)],
+        waits=(wait,),
+    )
+
+
+def sum_along_y(keep, give):
+    return keep + permute(give, Y_SWAP).astype(F32)
+
+
+def expert_end_kernel(
+    came_ref,
+    mid_ref,
+    cot_ref,
+    router_ref,
+    gain_ref,
+    hit_ref,
+    wout_ref,
+    dmid_ref,
+    low_ref,
+    datt_ref,
+    small_ref,
+):
+    dmoe_in = sum(came_ref[chip, :TPD].astype(F32) for chip in range(CHIPS))
+    rows = []
+    for chip in range(CHIPS):
+        lanes = came_ref[chip, TPD:].astype(F32)[:1]
+        for k in range(4):
+            rows.append(
+                lanes[:, 2 * k * TPD : (2 * k + 1) * TPD]
+                + lanes[:, (2 * k + 1) * TPD : (2 * k + 2) * TPD]
+            )
+    route_grad = jnp.concatenate(rows, axis=0)
+    mid = mid_ref[...]
+    scale = rms_scale(mid)
+    hat = mid * scale
+    gain = gain_ref[...]
+    rows_in = (hat * gain).astype(BF16)
+    router = router_ref[...]
+    gate = routed_softmax(mm(router, rows_in, 1, 1), hit_ref[...] > 0)
+    dlogits = gate * (route_grad - jnp.sum(gate * route_grad, axis=0, keepdims=True))
+    dlogits = dlogits.astype(BF16)
+    dmoe_in = dmoe_in + mm(dlogits, router, 0, 0)
+    small_ref[:EXPERTS] = mm(dlogits, rows_in, 1, 0)
+    small_ref[EXPERTS:] = jnp.broadcast_to(
+        jnp.sum(dmoe_in * hat, axis=0, keepdims=True), (8, D)
+    )
+    dmid = cot_ref[...].astype(F32) + norm_back(dmoe_in * gain, hat, scale)
+    dmid_ref[...] = dmid
+    low = dmid.astype(BF16)
+    low_ref[...] = low
+    datt = mm(wout_ref[...].reshape(HEADS * HD, D), low, 1, 1)
+    datt_ref[...] = datt.astype(BF16).reshape(SHARDS, HD, TPD)
+
+
+def out_kernel(core_ref, att_ref, first_ref, second_ref, keep_ref, give_ref):
+    att = att_ref[...]
+    total = mm(att[:, :TPD], first_ref[...], 1, 0) + mm(att[:, TPD:], second_ref[...], 1, 0)
+    total = total.astype(BF16).reshape(CHIPS, 2, D // SHARDS, D)
+    for core in range(2):
+
+        @pl.when(core_ref[0] == core)
+        def put(core=core):
+            keep_ref[...] = total[:, core]
+            give_ref[...] = total[:, 1 - core]
+
+
+def input_kernel(dproj_ref, left_ref, right_ref, x_ref, dmid_ref, gain_ref, out_ref):
+    queries = dproj_ref[:, :HD, :].reshape(HEADS * HD, TPD)
+    paired = dproj_ref[:, HD:, :].astype(F32).reshape(KV_HEADS, 2, 2 * HD, TPD)
+    paired = (paired[:, 0] + paired[:, 1]).astype(BF16)
+    both = [paired[:, :HD].reshape(KV_HEADS * HD, TPD), paired[:, HD:].reshape(KV_HEADS * HD, TPD)]
+    grad = mm(left_ref[...].reshape(D, D), queries, 1, 0)
+    grad = grad + mm(right_ref[...].reshape(D, D), jnp.concatenate(both, axis=0), 1, 0)
+    x = x_ref[...].astype(F32)
+    scale = rms_scale(x)
+    grad = norm_back(grad.T * gain_ref[...], x * scale, scale)
+    out_ref[...] = (dmid_ref[...] + grad).astype(BF16)
+
+
+def pack_kernel(ha_ref, hb_ref, sa_ref, sb_ref, ga_ref, gb_ref, out_ref):
+    small = sa_ref[...] + sb_ref[...]
+    gains = ga_ref[...] + gb_ref[...]
+    lane = lax.broadcasted_iota(jnp.int32, (HD, D), 1)
+    place = lax.broadcasted_iota(jnp.int32, (HD, D), 0)
+    four = HD // SHARDS
+    there = lane == place // four * (D // SHARDS) + place % four
+    rows = [
+        jnp.sum(jnp.where(there, gain[:, :1], 0.0), axis=0, keepdims=True)
+        for gain in (gains[:HD], gains[HD:])
+    ]
+    rows = jnp.concatenate(
+        [
+            ha_ref[...] + hb_ref[...],
+            small[: EXPERTS + 1],
+            *rows,
+            jnp.zeros((PACK - HEAD_COLS - EXPERTS - 3, D), F32),
+        ],
+        axis=0,
+    )
+    out_ref[...] = rows.T.astype(BF16).reshape(SHARDS, D // SHARDS, PACK)
+
+
+def own_kernel(got_ref, keep_ref, came_ref, out_ref):
+    left = lax.broadcasted_iota(jnp.int32, (D // SHARDS, TPD), 1) < HD
+    swap = lambda v: pltpu.roll(v, HD, 1)
+    query_key = [got_ref[h, :, :TPD].astype(F32) for h in range(HEADS)]
+    value_rest = [got_ref[h, :, TPD:].astype(F32) for h in range(HEADS)]
+    pairs = range(0, HEADS, 2)
+    queries = [jnp.where(left, query_key[h], swap(query_key[h + 1])) for h in pairs]
+    keys = [query_key[h] + query_key[h + 1] for h in pairs]
+    values = [value_rest[h] + value_rest[h + 1] for h in pairs]
+    rest = sum(values)
+    keys = [jnp.where(left, swap(keys[h]), keys[h + 1]) for h in range(0, KV_HEADS, 2)]
+    values = [jnp.where(left, values[h], swap(values[h + 1])) for h in range(0, KV_HEADS, 2)]
+    out = keep_ref[...] + came_ref[...].astype(F32)
+    out_ref[...] = jnp.concatenate([*queries, *keys, *values, out, rest], axis=1).astype(BF16)
+
+
+def share_kernel(parts_ref, out_ref):
+    total = sum(parts_ref[rep].astype(F32) for rep in range(REPS)).astype(BF16)
+    out_ref[...] = jnp.broadcast_to(total[None], out_ref.shape)
+
+
+def last_kernel(all_ref, wqkv_ref, gain_ref, qkv_ref, out_ref, rest_ref):
+    width = wqkv_ref.shape[1]
+    rows = all_ref[...].astype(F32).reshape(D // SHARDS, -1)
+    qkv_ref[...] = rows[:, :width]
+    out_ref[...] = rows[:, width : width + D]
+    gain = jnp.sum(rows[:, :width] * wqkv_ref[...].astype(F32), axis=1, keepdims=True)
+    left = lax.broadcasted_iota(jnp.int32, (D // SHARDS, TPD), 1) < HD
+    rest_ref[...] = jnp.where(left, gain / gain_ref[...], rows[:, width + D :])
 
 
 def local(
@@ -533,182 +776,204 @@
     tables = tables.reshape(MICRO, -1, CHUNKS, CHUNK).transpose(0, 2, 1, 3)
     for ready in (flat, tables):
         x_all = after(x_all, ready)
-    grads_all = gather(after(jnp.concatenate([cotangent, extra, w_out], axis=0), x_all))
-    hits_all = grads_all[:, MICRO * TPD : MICRO * TPD + 16]
-    hits_all = hits_all.reshape(SHARDS, 2 * MICRO, EXPERTS, TPD)[ordered]
-    out_full = grads_all[:, MICRO * TPD + 16 :].reshape(q_width, D)
+    packet = jnp.concatenate([micro(cotangent, 0), w_out, extra], axis=0)
+    packet = gather(after(packet, x_all))
+    hits_all = packet[:, TPD + own_rows :].reshape(SHARDS, 2 * MICRO, EXPERTS, TPD)
+    hits_all = hits_all[:, :MICRO][ordered].transpose(1, 0, 2, 3)
+    before = jnp.einsum("mset,tu->mseu", hits_all, earlier, preferred_element_type=F32)
+    slot_all = jnp.where(hits_all > 0, before, -1.0)
+    experts_own = shard * LOCAL_EXPERTS
+    slot_all = lax.dynamic_slice_in_dim(slot_all, experts_own, LOCAL_EXPERTS, 2)
+    slot_all = slot_all.transpose(0, 2, 1, 3)
     attn_in_all, raw, key, keyt, val, query, out, outf, inv = attn_fwd(
         x_all, w_head, attn_gain, query_gain, key_gain, tables
     )
-    attended = after(exchange(out), grads_all).reshape(q_width, MICRO * TPD)
-    x = block_input.astype(F32)
-    mid = x + mm(attended, out_full, 0, 0)
-    moe_scale = rms_scale(mid)
-    moe_hat = mid * moe_scale
-    moe_in = (moe_hat * moe_gain).astype(BF16)
-    rows_all = [gather_cores(micro(moe_in, 0)), (gather(micro(moe_in, 1)),)]
-
-    experts_own = shard * LOCAL_EXPERTS
+    attended = after(after(exchange(out), packet), slot_all).reshape(q_width, MICRO * TPD)
+    mid, rows_first, rows_second = call(
+        mid_kernel,
+        "mid",
+        [((MICRO * TPD, D), F32), ((CHIPS, TPD, D), BF16), ((3 * TPD, D), BF16)],
+        attended,
+        packet,
+        block_input,
+        moe_gain,
+        cotangent,
+        w_qkv,
+        specs={1: OUT_ROWS},
+    )
+    rows_first = exchange(rows_first, groups=SAME_CORE)
+    rows_first = (rows_first, permute(rows_first, OTHER_CORE))
+    rows_second = gather(rows_second)
+
+    own_experts = jnp.stack([core, experts_own])
+    router_rows = router.T
     grads, sums, chips = None, [], []
     for m in range(MICRO):
-        hit = hits_all[:, m]
-        before = jnp.einsum("set,tu->seu", hit, earlier, preferred_element_type=F32)
-        slot = jnp.where(hit > 0, before, -1.0)
-        slot = lax.dynamic_slice_in_dim(slot, experts_own, LOCAL_EXPERTS, 1).transpose(1, 0, 2)
-        if m == 1:
-            logits = mm(router, rows_all[1][0].reshape(G, D), 0, 1)
-            logits = logits.reshape(EXPERTS, SHARDS, TPD)[:, ordered].reshape(EXPERTS, G)
-        else:
-            logits = jnp.stack(
-                [mm(router, rows.reshape(G // 2, D), 0, 1) for rows in rows_all[m]], axis=1
-            ).reshape(EXPERTS, 2, CHIPS, TPD)
-            logits = logits.transpose(0, 2, 1, 3).reshape(EXPERTS, G)
-        gate = routed_softmax(logits, hit.transpose(1, 0, 2).reshape(EXPERTS, G) > 0)
-        gate = lax.dynamic_slice_in_dim(gate, experts_own, LOCAL_EXPERTS, 0)
-        *parts, route, g_gate, g_up, g_down = experts_step(
+        *parts, g_gate, g_up, g_down = experts_step(
             (chips[0],) if m else (),
-            m,
-            core.reshape(1),
-            rows_all[m],
-            grads_all,
-            slot,
-            gate.reshape(LOCAL_EXPERTS, SHARDS, TPD),
+            own_experts,
+            (rows_second,) if m else rows_first,
+            rows_second if m else packet,
+            slot_all[m],
+            hits_all[m].astype(F32),
+            router_rows,
             w_gate,
             w_up,
             w_down,
             grads,
         )
         grads = (g_gate, g_up, g_down)
-        sums.append((parts[:2], route))
+        sums.append(parts)
         if m == 0:
             chips.append(sum_cores(*parts[2:]))
-            qkv_full = lax.all_gather(after(w_qkv, route), "shard", axis=0, tiled=True)
-    grad_experts = lax.psum(tuple(grads), "rep")
-
-    out_part = jnp.zeros((q_width, D), F32)
-    small_part = jnp.zeros((D, EXPERTS + 1), F32)
-    grad_mid, grad_attended, back_attn = [], [], []
-    for m in range(MICRO):
-        route = sums[m][1]
-        scale, hat, rows_in = (micro(v, m) for v in (moe_scale, moe_hat, moe_in))
-        route_grad = exchange(route.transpose(1, 0, 2)[ordered]).reshape(EXPERTS, TPD)
-        came = exchange(chips[m], groups=SAME_CORE)
-        if m:
-            came = after(came, back_attn[0][0])
-        dmoe_in = jnp.sum(came.astype(F32), axis=0)
-        gate = routed_softmax(mm(router, rows_in, 0, 1), hits[m])
-        dlogits = gate * (route_grad - jnp.sum(gate * route_grad, axis=0, keepdims=True))
-        dlogits = dlogits.astype(BF16)
-        dmoe_in = dmoe_in + mm(dlogits, router, 0, 1)
-        moe_part = jnp.sum(dmoe_in * hat, axis=0)
-        small_part = small_part + jnp.concatenate(
-            [mm(rows_in, dlogits, 0, 1), moe_part[:, None]], axis=1
+            came = exchange(chips[0], groups=SAME_CORE)
+    grad_experts = lax.psum(tuple(after(grad, came) for grad in grads), "rep")
+
+    def expert_end(m, came):
+        rows = block((TPD, D), m, 0)
+        return call(
+            expert_end_kernel,
+            "expert_end",
+            [
+                ((TPD, D), F32),
+                ((TPD, D), BF16),
+                ((SHARDS, HD, TPD), BF16),
+                ((EXPERTS + 8, D), F32),
+            ],
+            came,
+            mid,
+            cotangent,
+            router_rows,
+            moe_gain,
+            hits[m].astype(F32),
+            packet,
+            specs={1: rows, 2: rows, 6: OUT_ROWS},
         )
-        dmid = micro(cotangent, m).astype(F32) + norm_back(dmoe_in * moe_gain, hat, scale)
-        low = dmid.astype(BF16)
-        out_part = out_part + mm(attended[:, m * TPD : (m + 1) * TPD], low, 1, 0)
-        dattended = mm(out_full, low, 1, 1).astype(BF16)
-        grad_mid.append(dmid)
-        grad_attended.append(exchange(dattended.reshape(SHARDS, HD, TPD)))
-        if m == 0:
-            chips.append(sum_cores(after(parts[2], grad_attended[0]), parts[3]))
-            grad_attended[0] = after(grad_attended[0], chips[1])
-        back_attn.append(
-            attn_bwd(
-                m,
-                grad_attended[m],
-                outf,
-                inv,
-                key,
-                keyt,
-                val,
-                query,
-                raw,
-                attn_in_all,
-                query_gain,
-                key_gain,
-                tables,
+
+    def attention_back(m, grad):
+        return attn_bwd(
+            m,
+            grad,
+            outf,
+            inv,
+            key,
+            keyt,
+            val,
+            query,
+            raw,
+            attn_in_all,
+            query_gain,
+            key_gain,
+            tables,
+        )
+
+    dmid_first, low_first, dattended, small_first = expert_end(0, came)
+
+    def rest():
+        grad_first = exchange(dattended)
+        chip = sum_cores(*sums[1][2:])
+        outs = sum_cores_by_x([parts[:2] for parts in sums], shard)
+        chip = after(chip, grad_first)
+        came = exchange(chip, groups=SAME_CORE)
+        for ready in (chip, outs[0]):
+            grad_first = after(grad_first, ready)
+        dproj_first, head_first, gains_first = attention_back(0, grad_first)
+        came = after(came, dproj_first)
+        dmid_second, low_second, second, small_second = expert_end(1, came)
+        second = exchange(second)
+        keep, give = call(
+            out_kernel,
+            "out_part",
+            [((CHIPS, own_rows, D), BF16)] * 2,
+            attended,
+            low_first,
+            low_second,
+            scalars=[core.reshape(1)],
+        )
+        out_own = sum_cores_by_x([(keep, give)], shard)
+        dproj_first = after(after(dproj_first, second), out_own[0])
+        outs = send_along_x(outs, second)
+        out_own = send_along_x(out_own, second)
+        second = after(second, dproj_first)
+        dproj_second, head_second, gains_second = attention_back(1, second)
+        dproj_first = exchange(dproj_first)
+        outs = sum_along_x(outs, shard, dproj_second)
+        keep, give = sum_along_x(out_own, shard, dproj_second)
+        (packed,) = call(
+            pack_kernel,
+            "pack",
+            [((SHARDS, own_rows, PACK), BF16)],
+            head_first,
+            head_second,
+            small_first,
+            small_second,
+            gains_first,
+            gains_second,
+        )
+        dproj_second = exchange(after(dproj_second, dproj_first))
+        dproj_all = [dproj_first, dproj_second]
+        for ready in (keep, outs[0], dproj_second):
+            packed = after(packed, ready)
+        packed = exchange(packed)
+        output = (mid + sum_along_y(*outs).reshape(mid.shape)).astype(BF16)
+        input_grads = []
+        for m in range(MICRO):
+            rows = block((TPD, D), m, 0)
+            input_grads += call(
+                input_kernel,
+                "input_grad",
+                [((TPD, D), BF16)],
+                dproj_all[m],
+                rows_second,
+                rows_second,
+                block_input,
+                (dmid_first, dmid_second)[m],
+                attn_gain,
+                specs={
+                    1: block((SHARDS, own_rows, D), 0, 4, 0),
+                    2: block((SHARDS, own_rows, D), 0, 5, 0),
+                    3: rows,
+                },
             )
+        width = q_width + 2 * kv_width
+        (owned,) = call(
+            own_kernel,
+            "own",
+            [((own_rows, width + D + TPD), BF16)],
+            packed,
+            keep[0],
+            permute(give, Y_SWAP)[0],
         )
-    blocks = out_part.astype(BF16).reshape(CHIPS, 2, own_rows, D)
-    out_own = sum_by_permutes(
-        lax.dynamic_index_in_dim(blocks, core, 1, keepdims=False),
-        lax.dynamic_index_in_dim(blocks, 1 - core, 1, keepdims=False),
-        shard,
-    )
-
-    outputs = []
-    for m in range(MICRO):
-        keep, give = sums[m][0]
-        total = sum_by_permutes(keep, after(give, grad_attended[1]), shard)
-        outputs.append((micro(mid, m) + total).astype(BF16))
-
-    input_grads = []
-    attn_part = jnp.zeros((D,), F32)
-    head_part = jnp.zeros((HEAD_COLS, D), F32)
-    gain_part = jnp.zeros((2 * HD,), F32)
-    for m in range(MICRO):
-        dproj, head_grad, gains = back_attn[m]
-        head_part = head_part + head_grad
-        gain_part = gain_part + gains[:, 0]
-        dproj = exchange(dproj if m else after(dproj, grad_attended[1]))
-        paired = dproj[:, HD:].astype(F32).reshape(KV_HEADS, 2, 2, HD, TPD).sum(axis=1)
-        dproj = jnp.concatenate(
-            [
-                dproj[:, :HD].reshape(q_width, TPD),
-                paired[:, 0].reshape(kv_width, TPD).astype(BF16),
-                paired[:, 1].reshape(kv_width, TPD).astype(BF16),
-            ],
-            axis=0,
+        owned = exchange(owned.reshape(REPS, own_rows // REPS, -1), "rep")
+        (share,) = call(
+            share_kernel, "share", [(owned.shape, BF16)], owned, waits=(output,)
         )
-        here = micro(x, m)
-        scale = rms_scale(here)
-        hat = here * scale
-        dattn_in = mm(dproj, qkv_full, 0, 1)
-        attn_part = attn_part + jnp.sum(dattn_in * hat, axis=0)
-        dx = grad_mid[m] + norm_back(dattn_in * attn_gain, hat, scale)
-        input_grads.append(dx.astype(BF16))
-
-    fours = gain_part.reshape(2, SHARDS, HD // SHARDS).transpose(1, 2, 0)
-    fours = jnp.pad(fours, ((0, 0), (0, own_rows - HD // SHARDS), (0, 0))).reshape(D, 2)
-    packed = jnp.concatenate([head_part.T, small_part, attn_part[:, None], fours], axis=1)
-    packed = jnp.pad(packed, ((0, 0), (0, PACK - packed.shape[1]))).astype(BF16)
-    for output in outputs:
-        packed = after(packed, output)
-    got = exchange(packed.reshape(SHARDS, own_rows, PACK)).astype(F32)
-    flat = lambda part: part.transpose(1, 0, 2).reshape(own_rows, -1)
-    pair_sum = lambda part: flat(part.reshape(KV_HEADS, 2, own_rows, HD).sum(axis=1))
-    owned = jnp.concatenate(
-        [
-            flat(got[:, :, :HD]),
-            pair_sum(got[:, :, HD : 2 * HD]),
-            pair_sum(got[:, :, 2 * HD : HEAD_COLS]),
-            out_own.astype(F32),
-            got[:, :, HEAD_COLS:].sum(axis=0),
-            jnp.zeros((own_rows, HD), F32),
-        ],
-        axis=1,
-    ).astype(BF16)
-    width = owned.shape[1]
-    share = jnp.sum(
-        exchange(owned.reshape(REPS, own_rows // REPS, width), "rep").astype(F32), axis=0
-    ).astype(BF16)
-    owned = exchange(jnp.broadcast_to(share[None], (REPS, *share.shape)), "rep")
-    owned = owned.reshape(own_rows, width).astype(F32)
-    base = q_width + 2 * kv_width + D
-    four = HD // SHARDS
-    return (
-        jnp.concatenate(outputs, axis=0),
-        jnp.concatenate(input_grads, axis=0),
-        owned[:, : base - D],
-        owned[:, base - D : base],
-        owned[:, base : base + EXPERTS],
-        owned[:, base + EXPERTS + 1],
-        owned[:, base + EXPERTS],
-        owned[:four, base + EXPERTS + 2],
-        owned[:four, base + EXPERTS + 3],
-        *(g.astype(F32) for g in grad_experts),
-    )
+        grad_qkv, grad_out, rest = call(
+            last_kernel,
+            "last",
+            [((own_rows, width), F32), ((own_rows, D), F32), ((own_rows, TPD), F32)],
+            exchange(share, "rep"),
+            w_qkv,
+            g_attn.astype(F32)[:, None],
+        )
+        four = HD // SHARDS
+        return (
+            output,
+            jnp.concatenate(input_grads, axis=0),
+            grad_qkv,
+            grad_out,
+            rest[:, HD : HD + EXPERTS],
+            rest[:, 0],
+            rest[:, HD + EXPERTS],
+            rest[:four, HD + EXPERTS + 1],
+            rest[:four, HD + EXPERTS + 2],
+        )
+
+    def none():
+        return jax.tree.map(lambda v: jnp.zeros(v.shape, v.dtype), jax.eval_shape(rest))
+
+    results = lax.cond(lengths[0, 0, 0] > 0, rest, none)
+    return (*results, *(g.astype(F32) for g in grad_experts))
 
 
 def solution(mesh):

time: 589 us -> 533 us (0.905)
  Pallas kernels: 133 us -> 196 us
  other arithmetic: 53.7 us -> 20 us
  matrix products: 28.5 us -> 0.21 us
  waiting for transfers between devices: 154 us -> 132 us
  local copies, waits for them, and re-layouts: 50.8 us -> 30.6 us
  starting transfers between devices: 86.7 us -> 72.8 us
    pallas_call x0 -> x16, Pallas kernels: none -> 60.7 us  [the longest x12 41.4 us: call(): pl.pallas_call(body, grid_spec=pltpu.PrefetchScalarGridSpec(num_scalar_pr...]
    dot_general x18 -> x1, matrix products: 28.5 us -> 0.21 us  [local(): jnp.einsum('mset,tu->mseu', hits_all, earlier, preferred_element_type=F32)]
    convert_element_type x16 -> x7, other arithmetic: 30.7 us -> 12.5 us  [the longest x3 9.44 us: local(): return (*results, *(g.astype(F32) for g in grad_experts))]
    all_to_all x12 -> x10, starting transfers between devices: 63.3 us -> 51.7 us  [exchange(): lax.all_to_all(values, axis, split_axis=0, concat_axis=0, tiled=True, axi...]
    slice x14 -> x7, local copies, waits for them, and re-layouts: 16.6 us -> 5.28 us  [the longest x1 1.08 us: local(): packet[:, TPD + own_rows:].reshape(SHARDS, 2 * MICRO, EXPERTS, TPD)]
    all_to_all x12 -> x10, waiting for transfers between devices: 40.8 us -> 30.6 us  [exchange(): lax.all_to_all(values, axis, split_axis=0, concat_axis=0, tiled=True, axi...]
    all_gather x3, waiting for transfers between devices: 59.1 us -> 49.9 us  [gather(): return lax.all_gather(values, 'shard', axis=0)]
    reduce_sum x14 -> x0, other arithmetic: 8.67 us -> none  [the longest x2 4.89 us: local(): dmoe_in = jnp.sum(came.astype(F32), axis=0)]
  transfers between devices with their start and end apart: 35 -> 28, of which waited for: 17 -> 12; matrix products, arithmetic and copies ran while one was open for 20% -> 6% of each run, Pallas kernels for 23% -> 37%
where the time goes in v2:
time: 533 us; the launch traced here: 524 us
  Pallas kernels  196 us (37%)
  waiting for transfers between devices  132 us (25%)
  starting transfers between devices  72.8 us (14%)
  blocking collectives  56.6 us (11%)
  local copies, waits for them, and re-layouts  30.6 us (6%)
  other arithmetic  20 us (4%)
  between operations  15.2 us (3%)
    pallas_call x2, Pallas kernels, experts_step(): pl.pallas_call(functools.partial(expert_kernel, later=later, kinds=kinds,...  61.4 us
    all_to_all x2, blocking collectives, exchange(): lax.all_to_all(values, axis, split_axis=0, concat_axis=0, tiled=True, axi...  56.6 us
    all_to_all x10, starting transfers between devices, exchange(): lax.all_to_all(values, axis, split_axis=0, concat_axis=0, tiled=True, axi...  51.7 us
    ppermute x14, waiting for transfers between devices, permute(): return lax.ppermute(values, 'shard', pairs)  50.4 us
    all_gather x3, waiting for transfers between devices, gather(): return lax.all_gather(values, 'shard', axis=0)  49.9 us
    pallas_call x2, Pallas kernels, attn_bwd(): pl.pallas_call(attn_bwd_kernel, grid=(1,), in_specs=[whole(*grad.shape)]...  42.9 us
    pallas_call x12, Pallas kernels, call(): pl.pallas_call(body, grid_spec=pltpu.PrefetchScalarGridSpec(num_scalar_pr...  41.4 us
    pallas_call x1, Pallas kernels, attn_fwd(): pl.pallas_call(attn_fwd_kernel, grid=(MICRO, CHUNKS), in_specs=[pl.BlockS...  31 us
  transfers between devices with their start and end apart: 28, of which 12 were waited for; matrix products, arithmetic and copies ran while one was open for 6% of the time, Pallas kernels for 37%

profile of v2, /device:TPU:1, one launch (start us, length us, event | category | flops | bytes accessed | tf_op | source)
XLA Modules:
  0.0 523.6 jit_solution(12895621746108047364)
XLA Ops:
  14.1 6.8 %all-to-all-start.8 = ((bf16[16,64,256]{2,1,0:T(8,128)(2,1)}), bf16[16,64,256]{2,1,0:T(8,128)(2,1)S(1)}, u32[]{:S(2)}, u32[]{:S(2)}) async-start(bf16[16,64,256]{2,1,0:T(8,128)(2,1)} %copy.116), calls=%async_computation.8 | async-start | bytes 1048576 | tf_op jit(solution)/shard_map/all_to_all | solution.py:452
  24.4 10.7 %all-to-all-done.8 = bf16[16,64,256]{2,1,0:T(8,128)(2,1)S(1)} async-done(((bf16[16,64,256]{2,1,0:T(8,128)(2,1)}), bf16[16,64,256]{2,1,0:T(8,128)(2,1)S(1)}, u32[]{:S(2)}, u32[]{:S(2)}) %all-to-all-start.8) | async-done | bytes 524320 | tf_op jit(solution)/shard_map/all_to_all | solution.py:452
  35.2 35.4 %all-gather.7.cloned.1.call-done = bf16[4096,1024]{1,0:T(8,128)(2,1)} async-done(((bf16[256,1024]{1,0:T(8,128)(2,1)}), bf16[4096,1024]{1,0:T(8,128)(2,1)}) %all-gather.7.cloned.1.call-update) | async-done | bytes 8388624 | tf_op jit(solution)/shard_map/all_gather | solution.py:420
  74.1 31.0 %attn_fwd.1 = (bf16[2,2048,1024]{2,1,0:T(8,128)(2,1)}, f32[2,8,128,256]{3,2,1,0:T(8,128)}, bf16[2,2048,128]{2,1,0:T(8,128)(2,1)}, bf16[2,8,64,256]{3,2,1,0:T(8,1...) custom-call(bf16[16,256,1024]{2,1,0:T(8,128)(2,1)} %after.43.x_ref.e, ...), custom_call_target="tpu_custom_call" | custom-call | flops 1000000 | bytes 1000000 | tf_op jit(solution)/shard_map/attn_fwd/pallas_call | solution.py:142
  105.1 5.1 all-to-all-start.9
  110.2 14.4 %all-gather.9.cloned.1.call-done = bf16[3328,1024]{1,0:T(8,128)(2,1)} async-done(((bf16[208,1024]{1,0:T(8,128)(2,1)}), bf16[3328,1024]{1,0:T(8,128)(2,1)}) %all-gather.9.cloned.1.call-update) | async-done | bytes 6815760 | tf_op jit(solution)/shard_map/all_gather | solution.py:420
  133.1 44.3 %all_to_all.53.refs_0_ = bf16[8,128,1024]{2,1,0:T(8,128)(2,1)S(1)} all-to-all(bf16[8,128,1024]{2,1,0:T(8,128)(2,1)} %get-tuple-element.184), channel_id=1, replica_groups={{0,2,4,6,8,10,12,14},{1,3,5,7,9,11,13,15},{16,18,20,22,24,26,28,30},{17..., dimensions={0} | all-to-all | bytes 4194304 | tf_op jit(solution)/shard_map/all_to_all | solution.py:452
  177.4 4.7 collective-permute-start.12
  186.2 30.3 %experts.2 = (bf16[8,128,1024]{2,1,0:T(8,128)(2,1)}, bf16[8,128,1024]{2,1,0:T(8,128)(2,1)}, bf16[8,144,1024]{2,1,0:T(8,128)(2,1)}, bf16[8,144,1024]{2,1,0:T(8,12...) custom-call(s32[2]{0:T(128)} %pad_add_fusion.1.core_ref, ...), custom_call_target="tpu_custom_call" | custom-call | flops 1000000 | bytes 1000000 | tf_op jit(solution)/shard_map/experts/pallas_call | solution.py:384
  216.8 4.5 collective-permute-done.13.refs_1_
  222.7 4.5 sum_cores.3.refs_0_
  232.7 31.1 %experts.3 = (bf16[8,128,1024]{2,1,0:T(8,128)(2,1)}, bf16[8,128,1024]{2,1,0:T(8,128)(2,1)}, bf16[8,144,1024]{2,1,0:T(8,128)(2,1)}, bf16[8,144,1024]{2,1,0:T(8,12...) custom-call(s32[2]{0:T(128)} %pad_add_fusion.1.core_ref, ...), custom_call_target="tpu_custom_call" | custom-call | flops 1000000 | bytes 1000000 | tf_op jit(solution)/shard_map/experts/pallas_call | solution.py:384
  267.9 4.9 expert_end.3
  272.8 234.4 %conditional.1 = (bf16[256,1024]{1,0:T(8,128)(2,1)}, bf16[256,1024]{1,0:T(8,128)(2,1)}, f32[64,2048]{1,0:T(8,128)}, f32[64,1024]{1,0:T(8,128)}, f32[64]{0:T(128)...) conditional(s32[]{:T(128)} %bitcast.14, () %tuple.16, (s32[]{:T(128)}, ...), branch_computations={%region_5.6_spmd, %region_6.7_spmd} | conditional | flops 34101344 | bytes 124955024 | solution.py:975
  273.4 7.8 %all-to-all-start = ((bf16[16,64,128]{2,1,0:T(8,128)(2,1)}), bf16[16,64,128]{2,1,0:T(8,128)(2,1)}, u32[]{:S(2)}, u32[]{:S(2)}) async-start(bf16[16,64,128]{2,1,0:T(8,128)(2,1)} %get-tuple-element.80), calls=%async_computation | async-start | bytes 524288 | tf_op jit(solution)/shard_map/cond/branch_1_fun/all_to_all | solution.py:452
  281.7 4.5 sum_cores.2.values_ref
  288.8 4.6 all-to-all-start.1
  295.4 6.9 %sum_cores_by_x.2 = (bf16[2,2,128,1024]{3,2,1,0:T(8,128)(2,1)}, bf16[2,2,128,1024]{3,2,1,0:T(8,128)(2,1)}, bf16[2,2,128,1024]{3,2,1,0:T(8,128)(2,1)}, bf16[2,2,128,1024]{3,2,1,0:T(8,128)(2,1)}) custom-call(s32[1]{0:T(128)} %bitcast.1.x_ref, bf16[2,4,128,1024]{3,2,1,0:T(8,128)(2,1)} %bitcast.112, bf16[2,4,128,1024]{3,2,1,0:T(8,128)(2,1)} %bitcast.3.refs_1_, ...), custom_call_target="tpu_custom_call" | custom-call | flops 1000000 | bytes 1000000 | tf_op jit(solution)/shard_map/cond/branch_1_fun/sum_cores_by_x/pallas_call | solution.py:541
  302.3 21.4 %attn_bwd.2 = (bf16[16,192,128]{2,1,0:T(8,128)(2,1)}, f32[192,1024]{1,0:T(8,128)}, f32[128,128]{1,0:T(8,128)}) custom-call(bf16[16,64,128]{2,1,0:T(8,128)(2,1)} %after.27.grad_ref, f32[2,8,64,256]{3,2,1,0:T(8,128)} %get-tuple-element.81.outf_ref, f32[2,8,1,256]{3,2,1,0:T(1,128)S(1)} %get-tuple-element.82.inv_ref, ...), custom_call_target="tpu_custom_call" | custom-call | flops 1000000 | bytes 1000000 | tf_op jit(solution)/shard_map/cond/branch_1_fun/attn_bwd/pallas_call | solution.py:247
  327.5 4.8 expert_end.2
  337.5 12.4 %all_to_all.52.earlier_ref.values_ref = bf16[16,64,128]{2,1,0:T(8,128)(2,1)} all-to-all(bf16[16,64,128]{2,1,0:T(8,128)(2,1)} %get-tuple-element.98), channel_id=1, replica_groups=mesh['rep'=8,'shard'=16] {'shard'}, dimensions={0} | all-to-all | bytes 524288 | tf_op jit(solution)/shard_map/cond/branch_1_fun/all_to_all | solution.py:452
  353.4 4.5 all-to-all-start.3
  363.0 21.5 %attn_bwd.3 = (bf16[16,192,128]{2,1,0:T(8,128)(2,1)}, f32[192,1024]{1,0:T(8,128)}, f32[128,128]{1,0:T(8,128)}) custom-call(bf16[16,64,128]{2,1,0:T(8,128)(2,1)} %after.34.grad_ref, f32[2,8,64,256]{3,2,1,0:T(8,128)} %get-tuple-element.81.outf_ref, f32[2,8,1,256]{3,2,1,0:T(1,128)S(1)} %get-tuple-element.82.inv_ref, ...), custom_call_target="tpu_custom_call" | custom-call | flops 1000000 | bytes 1000000 | tf_op jit(solution)/shard_map/cond/branch_1_fun/attn_bwd/pallas_call | solution.py:247
  386.6 4.7 all-to-all-start.4
  396.4 18.9 %collective-permute-done.4.refs_3_ = bf16[2,2,128,1024]{3,2,1,0:T(8,128)(2,1)} collective-permute-done((bf16[2,2,128,1024]{3,2,1,0:T(8,128)(2,1)}, bf16[2,2,128,1024]{3,2,1,0:T(8,128)(2,1)}, u32[]{:S(2)}, u32[]{:S(2)}) %collective-permute-start.4) | collective-permute-done | bytes 1048608 | tf_op jit(solution)/shard_map/cond/branch_1_fun/ppermute | solution.py:448
  423.2 7.0 %collective-permute-done.8.refs_2_ = bf16[1,2,64,1024]{3,2,1,0:T(8,128)(2,1)} collective-permute-done((bf16[1,2,64,1024]{3,2,1,0:T(8,128)(2,1)S(1)}, bf16[1,2,64,1024]{3,2,1,0:T(8,128)(2,1)}, u32[]{:S(2)}, u32[]{:S(2)}) %collective-permute-start.8) | collective-permute-done | bytes 262176 | tf_op jit(solution)/shard_map/cond/branch_1_fun/ppermute | solution.py:448
  430.1 4.9 collective-permute-done.9.refs_3_
  443.7 15.0 %collective-permute-done.11 = bf16[1,64,1024]{2,1,0:T(8,128)(2,1)S(1)} collective-permute-done((bf16[1,64,1024]{2,1,0:T(8,128)(2,1)}, bf16[1,64,1024]{2,1,0:T(8,128)(2,1)S(1)}, u32[]{:S(2)}, u32[]{:S(2)}) %collective-permute-start.11) | collective-permute-done | bytes 131104 | tf_op jit(solution)/shard_map/cond/branch_1_fun/ppermute | solution.py:448
  461.6 6.0 %all-to-all-start.6 = ((bf16[8,8,3200]{2,1,0:T(8,128)(2,1)}), bf16[8,8,3200]{2,1,0:T(8,128)(2,1)S(1)}, u32[]{:S(2)}, u32[]{:S(2)}) async-start(bf16[8,8,3200]{2,1,0:T(8,128)(2,1)} %bitcast.118), calls=%async_computation.6 | async-start | bytes 819200 | tf_op jit(solution)/shard_map/cond/branch_1_fun/all_to_all | solution.py:452
  470.0 13.4 %all-to-all-done.6.refs_0_ = bf16[8,8,3200]{2,1,0:T(8,128)(2,1)S(1)} async-done(((bf16[8,8,3200]{2,1,0:T(8,128)(2,1)}), bf16[8,8,3200]{2,1,0:T(8,128)(2,1)S(1)}, u32[]{:S(2)}, u32[]{:S(2)}) %all-to-all-start.6) | async-done | bytes 409632 | tf_op jit(solution)/shard_map/cond/branch_1_fun/all_to_all | solution.py:452
  490.1 4.7 input_grad.2
  494.8 4.8 input_grad.3
  (225 shorter events, 112.5 us)
Async XLA Ops:
  7.2 63.4 %all-gather.7.cloned.1.call-start = ((), (), s32[]{:S(2)}) async-start(), calls=%async_computation.12 | async-start | bytes 8912896 | tf_op jit(solution)/shard_map/all_gather | solution.py:420
  14.1 21.0 %all-to-all-start.8 = ((bf16[16,64,256]{2,1,0:T(8,128)(2,1)}), bf16[16,64,256]{2,1,0:T(8,128)(2,1)S(1)}, u32[]{:S(2)}, u32[]{:S(2)}) async-start(bf16[16,64,256]{2,1,0:T(8,128)(2,1)} %copy.116), calls=%async_computation.8 | async-start | bytes 1048576 | tf_op jit(solution)/shard_map/all_to_all | solution.py:452
  20.9 103.7 %all-gather.9.cloned.1.call-start = ((), (), s32[]{:S(2)}) async-start(), calls=%async_computation.13 | async-start | bytes 7241728 | tf_op jit(solution)/shard_map/all_gather | solution.py:420
  24.4 49.7 %copy-start.1 = (f32[2,8,80,256]{3,2,1,0:T(8,128)}, f32[2,8,80,256]{3,2,1,0:T(8,128)S(1)}, u32[]{:S(2)}) copy-start(f32[2,8,80,256]{3,2,1,0:T(8,128)S(1)} %maximum_bitcast_fusion.earlier_ref.tab_ref) | copy-start | bytes 3932164
  35.2 35.4 %copy-start.5 = (bf16[16,64,256]{2,1,0:T(8,128)(2,1)}, bf16[16,64,256]{2,1,0:T(8,128)(2,1)S(1)}, u32[]{:S(2)}) copy-start(bf16[16,64,256]{2,1,0:T(8,128)(2,1)S(1)} %all-to-all-done.8) | copy-start | bytes 1572868
  105.1 22.5 %all-to-all-start.9 = ((bf16[16,64,256]{2,1,0:T(8,128)(2,1)}), bf16[16,64,256]{2,1,0:T(8,128)(2,1)S(1)}, u32[]{:S(2)}, u32[]{:S(2)}) async-start(bf16[16,64,256]{2,1,0:T(8,128)(2,1)} %get-tuple-element.183), calls=%async_computation.9 | async-start | bytes 1048576 | tf_op jit(solution)/shard_map/all_to_all | solution.py:452
  110.2 122.5 %all-gather.11.cloned.1.call-start = ((), (), s32[]{:S(2)}) async-start(), calls=%async_computation.14 | async-start | bytes 13369344 | tf_op jit(solution)/shard_map/all_gather | solution.py:420
  177.4 8.8 %copy-start.4 = (bf16[8,128,1024]{2,1,0:T(8,128)(2,1)}, bf16[8,128,1024]{2,1,0:T(8,128)(2,1)S(1)}, u32[]{:S(2)}) copy-start(bf16[8,128,1024]{2,1,0:T(8,128)(2,1)S(1)} %all_to_all.53.refs_0_) | copy-start | bytes 6291460
  177.4 8.8 %collective-permute-start.12 = (bf16[8,128,1024]{2,1,0:T(8,128)(2,1)S(1)}, bf16[8,128,1024]{2,1,0:T(8,128)(2,1)}, u32[]{:S(2)}, u32[]{:S(2)}) collective-permute-start(bf16[8,128,1024]{2,1,0:T(8,128)(2,1)S(1)} %all_to_all.53.refs_0_), channel_id=1, source_target_pairs={{0,1},{1,0},{2,3},{3,2},{4,5},{5,4},{6,7},{7,6},{8,9},{9,8},{10,11... | collective-permute-start | bytes 6291464 | tf_op jit(solution)/shard_map/ppermute | solution.py:448
  216.5 4.8 collective-permute-start.13
  227.2 36.6 %all-to-all-start.11 = ((bf16[8,144,1024]{2,1,0:T(8,128)(2,1)}), bf16[8,144,1024]{2,1,0:T(8,128)(2,1)S(1)}, u32[]{:S(2)}, u32[]{:S(2)}) async-start(bf16[8,144,1024]{2,1,0:T(8,128)(2,1)} %sum_cores.3.refs_0_), calls=%async_computation.11 | async-start | bytes 4718592 | tf_op jit(solution)/shard_map/all_to_all | solution.py:452
  231.6 275.7 %all-reduce.7.cloned.1.call-start = ((), (), s32[]{:S(2)}) async-start(), calls=%async_computation.15 | async-start | bytes 12582912 | tf_op jit(solution)/shard_map/psum | solution.py:830
  272.8 8.9 %collective-permute-start.2 = (bf16[8,144,1024]{2,1,0:T(8,128)(2,1)}, bf16[8,144,1024]{2,1,0:T(8,128)(2,1)}, u32[]{:S(2)}, u32[]{:S(2)}) collective-permute-start(bf16[8,144,1024]{2,1,0:T(8,128)(2,1)} %get-tuple-element.79), channel_id=1, source_target_pairs={{0,1},{1,0},{2,3},{3,2},{4,5},{5,4},{6,7},{7,6},{8,9},{9,8},{10,11... | collective-permute-start | bytes 7077896 | tf_op jit(solution)/shard_map/cond/branch_1_fun/ppermute | solution.py:448
  273.4 15.4 %all-to-all-start = ((bf16[16,64,128]{2,1,0:T(8,128)(2,1)}), bf16[16,64,128]{2,1,0:T(8,128)(2,1)}, u32[]{:S(2)}, u32[]{:S(2)}) async-start(bf16[16,64,128]{2,1,0:T(8,128)(2,1)} %get-tuple-element.80), calls=%async_computation | async-start | bytes 524288 | tf_op jit(solution)/shard_map/cond/branch_1_fun/all_to_all | solution.py:452
  281.2 14.2 %collective-permute-start = (bf16[8,128,1024]{2,1,0:T(8,128)(2,1)}, bf16[8,128,1024]{2,1,0:T(8,128)(2,1)}, u32[]{:S(2)}, u32[]{:S(2)}) collective-permute-start(bf16[8,128,1024]{2,1,0:T(8,128)(2,1)} %get-tuple-element.73), channel_id=1, source_target_pairs={{0,1},{1,0},{2,3},{3,2},{4,5},{5,4},{6,7},{7,6},{8,9},{9,8},{10,11... | collective-permute-start | bytes 6291464 | tf_op jit(solution)/shard_map/cond/branch_1_fun/ppermute | solution.py:448
  281.4 14.0 %collective-permute-start.1 = (bf16[8,128,1024]{2,1,0:T(8,128)(2,1)}, bf16[8,128,1024]{2,1,0:T(8,128)(2,1)}, u32[]{:S(2)}, u32[]{:S(2)}) collective-permute-start(bf16[8,128,1024]{2,1,0:T(8,128)(2,1)} %get-tuple-element.75), channel_id=1, source_target_pairs={{0,1},{1,0},{2,3},{3,2},{4,5},{5,4},{6,7},{7,6},{8,9},{9,8},{10,11... | collective-permute-start | bytes 6291464 | tf_op jit(solution)/shard_map/cond/branch_1_fun/ppermute | solution.py:448
  288.8 38.8 %all-to-all-start.1 = ((bf16[8,144,1024]{2,1,0:T(8,128)(2,1)}), bf16[8,144,1024]{2,1,0:T(8,128)(2,1)}, u32[]{:S(2)}, u32[]{:S(2)}) async-start(bf16[8,144,1024]{2,1,0:T(8,128)(2,1)} %after.25.earlier_ref), calls=%async_computation.1 | async-start | bytes 4718592 | tf_op jit(solution)/shard_map/cond/branch_1_fun/all_to_all | solution.py:452
  336.1 13.8 %collective-permute-start.6 = (bf16[8,64,1024]{2,1,0:T(8,128)(2,1)}, bf16[8,64,1024]{2,1,0:T(8,128)(2,1)}, u32[]{:S(2)}, u32[]{:S(2)}) collective-permute-start(bf16[8,64,1024]{2,1,0:T(8,128)(2,1)} %get-tuple-element.106), channel_id=1, source_target_pairs={{0,1},{1,0},{2,3},{3,2},{4,5},{5,4},{6,7},{7,6},{8,9},{9,8},{10,11... | collective-permute-start | bytes 3145736 | tf_op jit(solution)/shard_map/cond/branch_1_fun/ppermute | solution.py:448
  353.4 33.2 %all-to-all-start.3 = ((bf16[16,192,128]{2,1,0:T(8,128)(2,1)}), bf16[16,192,128]{2,1,0:T(8,128)(2,1)}, u32[]{:S(2)}, u32[]{:S(2)}) async-start(bf16[16,192,128]{2,1,0:T(8,128)(2,1)} %after.33.earlier_ref), calls=%async_computation.3 | async-start | bytes 1572864 | tf_op jit(solution)/shard_map/cond/branch_1_fun/all_to_all | solution.py:452
  357.9 37.3 %collective-permute-start.3 = (bf16[2,2,128,1024]{3,2,1,0:T(8,128)(2,1)}, bf16[2,2,128,1024]{3,2,1,0:T(8,128)(2,1)}, u32[]{:S(2)}, u32[]{:S(2)}) collective-permute-start(bf16[2,2,128,1024]{3,2,1,0:T(8,128)(2,1)} %after.29), channel_id=1, source_target_pairs={{0,2},{1,3},{2,4},{3,5},{4,6},{5,7},{6,0},{7,1},{8,10},{9,11},{10,... | collective-permute-start | bytes 3145736 | tf_op jit(solution)/shard_map/cond/branch_1_fun/ppermute | solution.py:448
  359.4 55.9 %collective-permute-start.4 = (bf16[2,2,128,1024]{3,2,1,0:T(8,128)(2,1)}, bf16[2,2,128,1024]{3,2,1,0:T(8,128)(2,1)}, u32[]{:S(2)}, u32[]{:S(2)}) collective-permute-start(bf16[2,2,128,1024]{3,2,1,0:T(8,128)(2,1)} %after.30), channel_id=1, source_target_pairs={{0,4},{1,5},{2,6},{3,7},{4,0},{5,1},{6,2},{7,3},{8,12},{9,13},{10,... | collective-permute-start | bytes 3145736 | tf_op jit(solution)/shard_map/cond/branch_1_fun/ppermute | solution.py:448
  361.8 53.5 %collective-permute-start.5 = (bf16[2,2,128,1024]{3,2,1,0:T(8,128)(2,1)}, bf16[2,2,128,1024]{3,2,1,0:T(8,128)(2,1)}, u32[]{:S(2)}, u32[]{:S(2)}) collective-permute-start(bf16[2,2,128,1024]{3,2,1,0:T(8,128)(2,1)} %after.31), channel_id=1, source_target_pairs={{0,6},{1,7},{2,0},{3,1},{4,2},{5,3},{6,4},{7,5},{8,14},{9,15},{10,... | collective-permute-start | bytes 3145736 | tf_op jit(solution)/shard_map/cond/branch_1_fun/ppermute | solution.py:448
  386.6 50.5 %all-to-all-start.4 = ((bf16[16,192,128]{2,1,0:T(8,128)(2,1)}), bf16[16,192,128]{2,1,0:T(8,128)(2,1)S(1)}, u32[]{:S(2)}, u32[]{:S(2)}) async-start(bf16[16,192,128]{2,1,0:T(8,128)(2,1)} %after.35), calls=%async_computation.4 | async-start | bytes 1572864 | tf_op jit(solution)/shard_map/cond/branch_1_fun/all_to_all | solution.py:452
  391.4 38.8 %collective-permute-start.8 = (bf16[1,2,64,1024]{3,2,1,0:T(8,128)(2,1)S(1)}, bf16[1,2,64,1024]{3,2,1,0:T(8,128)(2,1)}, u32[]{:S(2)}, u32[]{:S(2)}) collective-permute-start(bf16[1,2,64,1024]{3,2,1,0:T(8,128)(2,1)S(1)} %copy-done.22), channel_id=1, source_target_pairs={{0,2},{1,3},{2,4},{3,5},{4,6},{5,7},{6,0},{7,1},{8,10},{9,11},{10,... | collective-permute-start | bytes 786440 | tf_op jit(solution)/shard_map/cond/branch_1_fun/ppermute | solution.py:448
  392.8 42.2 %collective-permute-start.9 = (bf16[1,2,64,1024]{3,2,1,0:T(8,128)(2,1)S(1)}, bf16[1,2,64,1024]{3,2,1,0:T(8,128)(2,1)}, u32[]{:S(2)}, u32[]{:S(2)}) collective-permute-start(bf16[1,2,64,1024]{3,2,1,0:T(8,128)(2,1)S(1)} %copy-done.23), channel_id=1, source_target_pairs={{0,4},{1,5},{2,6},{3,7},{4,0},{5,1},{6,2},{7,3},{8,12},{9,13},{10,... | collective-permute-start | bytes 786440 | tf_op jit(solution)/shard_map/cond/branch_1_fun/ppermute | solution.py:448
  395.2 39.8 %collective-permute-start.10 = (bf16[1,2,64,1024]{3,2,1,0:T(8,128)(2,1)}, bf16[1,2,64,1024]{3,2,1,0:T(8,128)(2,1)}, u32[]{:S(2)}, u32[]{:S(2)}) collective-permute-start(bf16[1,2,64,1024]{3,2,1,0:T(8,128)(2,1)} %after.38), channel_id=1, source_target_pairs={{0,6},{1,7},{2,0},{3,1},{4,2},{5,3},{6,4},{7,5},{8,14},{9,15},{10,... | collective-permute-start | bytes 786440 | tf_op jit(solution)/shard_map/cond/branch_1_fun/ppermute | solution.py:448
  419.2 48.4 %collective-permute-start.7 = (bf16[2,128,1024]{2,1,0:T(8,128)(2,1)}, bf16[2,128,1024]{2,1,0:T(8,128)(2,1)S(1)}, u32[]{:S(2)}, u32[]{:S(2)}) collective-permute-start(bf16[2,128,1024]{2,1,0:T(8,128)(2,1)} %get-tuple-element.110), channel_id=1, source_target_pairs={{0,8},{1,9},{2,10},{3,11},{4,12},{5,13},{6,14},{7,15},{8,0},{9,1},... | collective-permute-start | bytes 1572872 | tf_op jit(solution)/shard_map/cond/branch_1_fun/ppermute | solution.py:448
  438.0 20.7 %all-to-all-start.5 = ((bf16[16,64,256]{2,1,0:T(8,128)(2,1)}), bf16[16,64,256]{2,1,0:T(8,128)(2,1)S(1)}, u32[]{:S(2)}, u32[]{:S(2)}) async-start(bf16[16,64,256]{2,1,0:T(8,128)(2,1)} %after.41), calls=%async_computation.5 | async-start | bytes 1048576 | tf_op jit(solution)/shard_map/cond/branch_1_fun/all_to_all | solution.py:452
  442.3 16.5 %collective-permute-start.11 = (bf16[1,64,1024]{2,1,0:T(8,128)(2,1)}, bf16[1,64,1024]{2,1,0:T(8,128)(2,1)S(1)}, u32[]{:S(2)}, u32[]{:S(2)}) collective-permute-start(bf16[1,64,1024]{2,1,0:T(8,128)(2,1)} %get-tuple-element.126), channel_id=1, source_target_pairs={{0,8},{1,9},{2,10},{3,11},{4,12},{5,13},{6,14},{7,15},{8,0},{9,1},... | collective-permute-start | bytes 393224 | tf_op jit(solution)/shard_map/cond/branch_1_fun/ppermute | solution.py:448
  461.6 21.8 %all-to-all-start.6 = ((bf16[8,8,3200]{2,1,0:T(8,128)(2,1)}), bf16[8,8,3200]{2,1,0:T(8,128)(2,1)S(1)}, u32[]{:S(2)}, u32[]{:S(2)}) async-start(bf16[8,8,3200]{2,1,0:T(8,128)(2,1)} %bitcast.118), calls=%async_computation.6 | async-start | bytes 819200 | tf_op jit(solution)/shard_map/cond/branch_1_fun/all_to_all | solution.py:452
  469.0 21.1 %copy-start.21 = (f32[128,1024]{1,0:T(8,128)S(1)}, f32[128,1024]{1,0:T(8,128)}, u32[]{:S(2)}) copy-start(f32[128,1024]{1,0:T(8,128)} %get-tuple-element.113.refs_4_) | copy-start | bytes 1572868 | tf_op jit(solution)/shard_map/cond
  486.0 15.4 %all-to-all-start.7 = ((bf16[8,8,3200]{2,1,0:T(8,128)(2,1)}), bf16[8,8,3200]{2,1,0:T(8,128)(2,1)S(1)}, u32[]{:S(2)}, u32[]{:S(2)}) async-start(bf16[8,8,3200]{2,1,0:T(8,128)(2,1)} %share.1), calls=%async_computation.7 | async-start | bytes 819200 | tf_op jit(solution)/shard_map/cond/branch_1_fun/all_to_all | solution.py:452
  (35 other events, 136.1 us)
Sparse Core Ops, SparseCore 0:
  9.7 60.8 all-gather.6
  72.8 51.7 all-gather.8
  133.2 90.0 all-gather.10
  265.4 222.2 all-reduce.6
